TPU v7x, 256 devices: a whole 4x4x8 slice. The times are simulated.
256 devices in a mesh: brick: 32 (over x, z_lo, core), sub: 8 (over z_hi, y).
Axes of the slice: x: 4, y: 4, z: 8 (z_hi: 2, z_lo: 4; z = z_hi * 4 + z_lo), core: 2. Of those that a mesh axis runs over, the one named last changes fastest.
Arguments:
- populations: float32 [19, 128, 128, 128], P(None, 'brick', 'sub'), may hold values from -0.75 to 0.75
- solid: int32 [128, 128, 128], P('brick', 'sub'), may hold values 0 or 1
- boundary_pressure: float32 [8192], P(('brick', 'sub')), may hold values from -4 to 4
- block_col: int32 [8192], P(('brick', 'sub')), may hold values from 0 to 63, as said below
- block_dest: int32 [8192, 1], P(('brick', 'sub')), may hold values from 0 to 31; in each aligned block of 32 rows (0 to 31, 32 to 63, ...) at most 3 rows name the same one
- block_seg: int32 [8192], P(('brick', 'sub')), may hold values from 0 to 2047
- seg_pressure: float32 [524288], P(('brick', 'sub')), may hold values from -6 to 6
- seg_rate: float32 [524288], P(('brick', 'sub')), may hold values from 0.05 to 0.25
- seg_leak: float32 [524288], P(('brick', 'sub')), may hold values from 0.1 to 1
- profile_weights: float32 [524288, 128], P(('brick', 'sub')), may hold values from -12 to 12
- junc_members: int32 [4, 262144], P(None, ('brick', 'sub')), may hold values from 0 to 16383
- junc_arity: int32 [262144], P(('brick', 'sub')), may hold values from 2 to 4
- junc_res: float32 [4, 262144], P(None, ('brick', 'sub')), may hold values from 1 to 2
- junc_cross: float32 [4, 4, 262144], P(None, None, ('brick', 'sub')), may hold values from -0.3 to 0.3
Outputs:
- populations_out: float32 [19, 128, 128, 128], P(None, 'brick', 'sub')
- seg_pressure_out: float32 [524288], P(('brick', 'sub'))
- boundary_pressure_out: float32 [8192], P(('brick', 'sub'))
Inputs may be any that keep to these rules, and one draw needn't show every extreme that they name: `block_col`: within one device's 32 blocks the columns are distinct. `block_dest`: in one device's 32 blocks no brick index is named more than 3 times, and some device names one brick index exactly 3 times; every brick index is named somewhere. `junc_members`: A member numbered m lies on the device of the junction's brick index with sub index m // 2048, at local index m % 2048.
All inputs are finite; a program needn't handle non-finite values. No bound on the sum of `solid` on one device may be relied on, other than what follows from the above.
Results may differ from a plain program's by a relative error of at most 0.00011.
Values sent between devices are 32-bit elements; how exact they have to be, the bound alone decides.
A program may use at most 64 MiB of HBM per device.

v0:
```python
import jax
import jax.numpy as jnp
import numpy as np
from jax import lax
from jax.sharding import PartitionSpec as P

STEPS = 6
SLOTS = 3


VELOCITIES = np.array(
    [
        [0, 0, 0],
        [1, 0, 0],
        [-1, 0, 0],
        [0, 1, 0],
        [0, -1, 0],
        [0, 0, 1],
        [0, 0, -1],
        [1, 1, 0],
        [-1, -1, 0],
        [1, -1, 0],
        [-1, 1, 0],
        [1, 0, 1],
        [-1, 0, -1],
        [1, 0, -1],
        [-1, 0, 1],
        [0, 1, 1],
        [0, -1, -1],
        [0, 1, -1],
        [0, -1, 1],
    ]
)
OPPOSITE = np.array([0, 2, 1, 4, 3, 6, 5, 8, 7, 10, 9, 12, 11, 14, 13, 16, 15, 18, 17])
LATTICE_WEIGHTS = np.array([1.0 / 3.0] + [1.0 / 18.0] * 6 + [1.0 / 36.0] * 12)
RELAXATION = 1.25
DENSITY_SCALE = 0.1


def extended(block, sides, width):
    for axis, dim in sides:
        count = lax.axis_size(axis)
        forward = [(i, i + 1) for i in range(count - 1)]
        forward.append((count - 1, 0))
        backward = [(target, source) for source, target in forward]
        low = lax.ppermute(
            lax.slice_in_dim(block, block.shape[dim] - width, None, axis=dim), axis, forward
        )
        high = lax.ppermute(lax.slice_in_dim(block, 0, width, axis=dim), axis, backward)
        block = jnp.concatenate([low, block, high], axis=dim)
    return block


def lattice_tables():
    weights = jnp.asarray(LATTICE_WEIGHTS, jnp.float32)
    moment_rows = jnp.asarray(VELOCITIES.T * LATTICE_WEIGHTS[None, :], jnp.float32)
    directions = jnp.asarray(VELOCITIES, jnp.float32)
    return (weights, moment_rows, directions)


def collide(lattice, solid, boundary_mask, boundary_density):
    weights, moment_rows, directions = lattice_tables()
    highest = lax.Precision.HIGHEST
    density = 1.0 + jnp.einsum("i,ixyz->xyz", weights, lattice, precision=highest)
    momentum = jnp.einsum("ai,ixyz->axyz", moment_rows, lattice, precision=highest)
    velocity = momentum / density[None]
    projected = jnp.einsum("ia,axyz->ixyz", directions, velocity, precision=highest)
    speed_sq = jnp.sum(velocity * velocity, axis=0)
    shape_terms = 1.0 + 3.0 * projected + 4.5 * projected * projected - 1.5 * speed_sq[None]
    relaxed = lattice - RELAXATION * (lattice - (density[None] * shape_terms - 1.0))
    bounced = lattice[OPPOSITE]
    collided = jnp.where(solid[None] > 0, bounced, relaxed)
    imposed = boundary_density[None, :, :, None] * shape_terms - 1.0
    return jnp.where(boundary_mask[None, :, :, None], imposed, collided)


def solve_blocks(matrix, right):
    matrix_order = matrix.shape[0]
    rows = [matrix[row_index] for row_index in range(matrix_order)]
    sides = [right[row_index] for row_index in range(matrix_order)]
    for column in range(matrix_order):
        for row_index in range(column + 1, matrix_order):
            factor = rows[row_index][column] / rows[column][column]
            rows[row_index] = rows[row_index] - factor[None] * rows[column]
            sides[row_index] = sides[row_index] - factor[None] * sides[column]
    answer = [None] * matrix_order
    for row_index in reversed(range(matrix_order)):
        running = sides[row_index]
        for column in range(row_index + 1, matrix_order):
            running = running - rows[row_index][column][None] * answer[column]
        answer[row_index] = running / rows[row_index][row_index][None]
    return jnp.stack(answer)


def junction_matrix(resist, cross, live):
    members_max = resist.shape[0]
    identity = jnp.eye(members_max, dtype=jnp.float32)[:, :, None]
    symmetric = 0.5 * (cross + jnp.transpose(cross, (1, 0, 2)))
    coupled = live[:, None, :] * live[None, :, :] * symmetric
    return identity * resist[:, None, :] + (1.0 - identity) * coupled


def junction_flows(matrix, live, member_pressure):
    driven = live * member_pressure
    solved = solve_blocks(matrix, jnp.stack([driven, live], axis=1))
    first = solved[:, 0]
    second = solved[:, 1]
    junction_pressure = jnp.sum(live * first, axis=0) / jnp.sum(live * second, axis=0)
    return live * (first - junction_pressure[None] * second)


def local(
    populations,
    solid,
    boundary_pressure,
    block_col,
    block_dest,
    block_seg,
    seg_pressure,
    seg_rate,
    seg_leak,
    profile_weights,
    junc_members,
    junc_arity,
    junc_res,
    junc_cross,
):
    bricks = lax.axis_size("brick")
    components, cells_x, cells_y, cells_z = populations.shape
    seg_count = seg_pressure.shape[0]
    block_count = block_col.shape[0]
    flow_rows = jnp.asarray(VELOCITIES[:, 0] * LATTICE_WEIGHTS, jnp.float32)
    axial = jnp.einsum("i,ixyz->xyz", flow_rows, populations, precision=lax.Precision.HIGHEST)
    profiles = axial.reshape(cells_x * cells_y, cells_z)[block_col]
    targets = block_dest[:, 0]
    ordinal = jnp.arange(block_count)
    earlier_same = (targets[:, None] == targets[None, :]) & (ordinal[None, :] < ordinal[:, None])
    slot_of = jnp.sum(earlier_same.astype(jnp.int32), axis=1)
    position = targets * SLOTS + slot_of
    outgoing = jnp.zeros((bricks * SLOTS, cells_z), jnp.float32).at[position].set(profiles)
    labels = (
        jnp.full((bricks * SLOTS,), -1.0, jnp.float32)
        .at[position]
        .set(block_seg.astype(jnp.float32))
    )
    arrived, arrived_labels = (
        lax.all_to_all(
            outgoing.reshape(bricks, SLOTS, cells_z),
            "brick",
            split_axis=0,
            concat_axis=0,
            tiled=True,
        ),
        lax.all_to_all(
            labels.reshape(bricks, SLOTS), "brick", split_axis=0, concat_axis=0, tiled=True
        ),
    )
    coupled = arrived_labels.reshape(-1).astype(jnp.int32)
    present = coupled >= 0
    safe_ids = jnp.where(present, coupled, 0)
    flux = jnp.sum(profile_weights[safe_ids] * arrived.reshape(-1, cells_z), axis=1)
    inflow = jax.ops.segment_sum(jnp.where(present, flux, 0.0), safe_ids, num_segments=seg_count)
    members_max = junc_res.shape[0]
    links, arity, resist, cross = (junc_members, junc_arity, junc_res, junc_cross)
    live = (jnp.arange(members_max)[:, None] < arity[None, :]).astype(jnp.float32)
    matrix = junction_matrix(resist, cross, live)
    pressure = seg_pressure
    for step_index in range(STEPS):
        group_pressure = lax.all_gather(pressure, "sub", axis=0, tiled=True)
        flows = junction_flows(matrix, live, group_pressure[links])
        group_terms = jax.ops.segment_sum(
            -flows.reshape(-1), links.reshape(-1), num_segments=group_pressure.shape[0]
        )
        balance = lax.psum_scatter(group_terms, "sub", scatter_dimension=0, tiled=True)
        pressure = pressure + seg_rate * (balance + inflow - seg_leak * pressure)
    answer_back = jnp.where(present, pressure[safe_ids], 0.0).reshape(bricks, SLOTS)
    returned = lax.all_to_all(answer_back, "brick", split_axis=0, concat_axis=0, tiled=True)
    new_pressure = returned.reshape(-1)[position]
    hits = block_col[:, None] == jnp.arange(cells_x * cells_y)[None, :]
    boundary_mask = jnp.any(hits, axis=0).reshape(cells_x, cells_y)
    imposed_sum = jnp.sum(jnp.where(hits, boundary_pressure[:, None], 0.0), axis=0).reshape(
        cells_x, cells_y
    )
    boundary_density = jnp.where(boundary_mask, 1.0 + DENSITY_SCALE * imposed_sum, 1.0)
    lattice = populations
    for step_index in range(STEPS):
        collided = collide(lattice, solid, boundary_mask, boundary_density)
        padded = extended(collided, (("brick", 1), ("sub", 2)), 1)
        moved = jnp.stack(
            [
                padded[
                    component,
                    1 - int(VELOCITIES[component, 0]) : 1 - int(VELOCITIES[component, 0]) + cells_x,
                    1 - int(VELOCITIES[component, 1]) : 1 - int(VELOCITIES[component, 1]) + cells_y,
                ]
                for component in range(components)
            ]
        )
        lattice = jnp.stack(
            [
                jnp.roll(moved[component], int(VELOCITIES[component, 2]), axis=-1)
                for component in range(components)
            ]
        )
    return (lattice, pressure, new_pressure)


def solution(mesh):
    return jax.shard_map(
        local,
        mesh=mesh,
        in_specs=(
            P(None, "brick", "sub", None),
            P("brick", "sub", None),
            P(("brick", "sub")),
            P(("brick", "sub")),
            P(("brick", "sub"), None),
            P(("brick", "sub")),
            P(("brick", "sub")),
            P(("brick", "sub")),
            P(("brick", "sub")),
            P(("brick", "sub"), None),
            P(None, ("brick", "sub")),
            P(("brick", "sub")),
            P(None, ("brick", "sub")),
            P(None, None, ("brick", "sub")),
        ),
        out_specs=(P(None, "brick", "sub", None), P(("brick", "sub")), P(("brick", "sub"))),
        check_vma=False,
    )
```

profile of v0, /device:TPU:1, one launch (start us, length us, event | category | flops | bytes accessed | tf_op | source)
XLA Modules:
  0.0 1298.1 jit_solution(609235326588542771)
XLA Ops:
  22.1 37.6 %all_gather.18 = f32[16384]{0:T(1024)S(1)} all-gather(f32[2048]{0:T(1024)S(1)} %copy-done.17), channel_id=1, replica_groups=mesh['brick'=32,'sub'=8] {'sub'}, dimensions={0}, use_global_device_ids=true | all-gather | bytes 73728 | tf_op jit(solution)/shard_map/all_gather | solution.py:169
  59.7 23.0 %gather_fusion.6 = f32[4096]{0:T(1024)S(1)} fusion(f32[16384]{0:T(1024)S(1)} %all_gather.18, s32[4096]{0:T(1024)S(1)} %bitcast_clamp_fusion), kind=kCustom, calls=%fused_computation.6 | custom fusion | bytes 49152 | tf_op jit(solution)/shard_map/gather | solution.py:170
  83.6 22.5 %scatter_custom_fusion = f32[16384]{0:T(1024)} fusion(s32[4096]{0:T(1024)S(1)} %bitcast.897, f32[4096]{0:T(1024)S(1)} %fusion.98, f32[]{:T(128)} %constant.77.clone.1), kind=kCustom, calls=%fused_computation.435 | custom fusion | flops 4096 | bytes 65540 | tf_op jit(solution)/shard_map/scatter-add | solution.py:171
  148.1 64.6 %all-reduce.13.cloned.1.call-done = f32[16384]{0:T(1024)} async-done(((f32[16384]{0:T(1024)}), f32[16384]{0:T(1024)}) %all-reduce.13.cloned.1.call-update) | async-done | bytes 65552
  213.4 37.6 %all_gather.19 = f32[16384]{0:T(1024)S(1)} all-gather(f32[2048]{0:T(1024)S(1)} %fusion.186), channel_id=1, replica_groups=mesh['brick'=32,'sub'=8] {'sub'}, dimensions={0}, use_global_device_ids=true | all-gather | bytes 73728 | tf_op jit(solution)/shard_map/all_gather | solution.py:169
  251.0 23.0 %gather_fusion.8 = f32[4096]{0:T(1024)S(1)} fusion(f32[16384]{0:T(1024)S(1)} %all_gather.19, s32[4096]{0:T(1024)S(1)} %bitcast_clamp_fusion), kind=kCustom, calls=%fused_computation.9 | custom fusion | bytes 49152 | tf_op jit(solution)/shard_map/gather | solution.py:170
  274.3 22.6 %scatter_custom_fusion.4 = f32[16384]{0:T(1024)} fusion(s32[4096]{0:T(1024)} %bitcast.898, f32[4096]{0:T(1024)S(1)} %fusion.95, f32[]{:T(128)} %constant.77.clone.1), kind=kCustom, calls=%fused_computation.433 | custom fusion | flops 4096 | bytes 66048 | tf_op jit(solution)/shard_map/scatter-add | solution.py:171
  303.1 100.5 %all-reduce.15.cloned.1.call-done = f32[16384]{0:T(1024)} async-done(((f32[16384]{0:T(1024)}), f32[16384]{0:T(1024)}) %all-reduce.15.cloned.1.call-update) | async-done | bytes 65552
  404.3 37.6 %all_gather.20 = f32[16384]{0:T(1024)S(1)} all-gather(f32[2048]{0:T(1024)S(1)} %fusion.183), channel_id=1, replica_groups=mesh['brick'=32,'sub'=8] {'sub'}, dimensions={0}, use_global_device_ids=true | all-gather | bytes 73728 | tf_op jit(solution)/shard_map/all_gather | solution.py:169
  441.9 23.0 %gather_fusion.9 = f32[4096]{0:T(1024)S(1)} fusion(f32[16384]{0:T(1024)S(1)} %all_gather.20, s32[4096]{0:T(1024)S(1)} %bitcast_clamp_fusion), kind=kCustom, calls=%fused_computation.10 | custom fusion | bytes 49152 | tf_op jit(solution)/shard_map/gather | solution.py:170
  465.2 22.6 %scatter_custom_fusion.5 = f32[16384]{0:T(1024)} fusion(s32[4096]{0:T(1024)} %bitcast.899, f32[4096]{0:T(1024)S(1)} %fusion.92, f32[]{:T(128)} %constant.77.clone.1), kind=kCustom, calls=%fused_computation.431 | custom fusion | flops 4096 | bytes 66048 | tf_op jit(solution)/shard_map/scatter-add | solution.py:171
  494.4 100.2 %all-reduce.17.cloned.1.call-done = f32[16384]{0:T(1024)} async-done(((f32[16384]{0:T(1024)}), f32[16384]{0:T(1024)}) %all-reduce.17.cloned.1.call-update) | async-done | bytes 65552
  595.3 38.0 %all_gather.21 = f32[16384]{0:T(1024)S(1)} all-gather(f32[2048]{0:T(1024)S(1)} %fusion.180), channel_id=1, replica_groups=mesh['brick'=32,'sub'=8] {'sub'}, dimensions={0}, use_global_device_ids=true | all-gather | bytes 73728 | tf_op jit(solution)/shard_map/all_gather | solution.py:169
  633.2 23.0 %gather_fusion.10 = f32[4096]{0:T(1024)S(1)} fusion(f32[16384]{0:T(1024)S(1)} %all_gather.21, s32[4096]{0:T(1024)S(1)} %bitcast_clamp_fusion), kind=kCustom, calls=%fused_computation.11 | custom fusion | bytes 49152 | tf_op jit(solution)/shard_map/gather | solution.py:170
  656.6 22.6 %scatter_custom_fusion.6 = f32[16384]{0:T(1024)} fusion(s32[4096]{0:T(1024)} %bitcast.900, f32[4096]{0:T(1024)S(1)} %fusion.89, f32[]{:T(128)} %constant.77.clone.1), kind=kCustom, calls=%fused_computation.429 | custom fusion | flops 4096 | bytes 66048 | tf_op jit(solution)/shard_map/scatter-add | solution.py:171
  679.3 106.5 %all-reduce.19.cloned.1.call-done = f32[16384]{0:T(1024)} async-done(((f32[16384]{0:T(1024)}), f32[16384]{0:T(1024)}) %all-reduce.19.cloned.1.call-update) | async-done | bytes 65552
  786.5 37.6 %all_gather.22 = f32[16384]{0:T(1024)S(1)} all-gather(f32[2048]{0:T(1024)S(1)} %fusion.177), channel_id=1, replica_groups=mesh['brick'=32,'sub'=8] {'sub'}, dimensions={0}, use_global_device_ids=true | all-gather | bytes 73728 | tf_op jit(solution)/shard_map/all_gather | solution.py:169
  824.1 23.0 %gather_fusion.11 = f32[4096]{0:T(1024)S(1)} fusion(f32[16384]{0:T(1024)S(1)} %all_gather.22, s32[4096]{0:T(1024)S(1)} %bitcast_clamp_fusion), kind=kCustom, calls=%fused_computation.12 | custom fusion | bytes 49152 | tf_op jit(solution)/shard_map/gather | solution.py:170
  847.4 22.6 %scatter_custom_fusion.7 = f32[16384]{0:T(1024)} fusion(s32[4096]{0:T(1024)} %bitcast.901, f32[4096]{0:T(1024)S(1)} %fusion.86, f32[]{:T(128)} %constant.77.clone.1), kind=kCustom, calls=%fused_computation.427 | custom fusion | flops 4096 | bytes 66048 | tf_op jit(solution)/shard_map/scatter-add | solution.py:171
  882.9 93.8 %all-reduce.21.cloned.1.call-done = f32[16384]{0:T(1024)} async-done(((f32[16384]{0:T(1024)}), f32[16384]{0:T(1024)}) %all-reduce.21.cloned.1.call-update) | async-done | bytes 65552
  977.4 37.6 %all_gather.23 = f32[16384]{0:T(1024)S(1)} all-gather(f32[2048]{0:T(1024)S(1)} %fusion.174), channel_id=1, replica_groups=mesh['brick'=32,'sub'=8] {'sub'}, dimensions={0}, use_global_device_ids=true | all-gather | bytes 73728 | tf_op jit(solution)/shard_map/all_gather | solution.py:169
  1015.0 23.0 %gather_fusion.12 = f32[4096]{0:T(1024)S(1)} fusion(f32[16384]{0:T(1024)S(1)} %all_gather.23, s32[4096]{0:T(1024)S(1)} %bitcast_clamp_fusion), kind=kCustom, calls=%fused_computation.13 | custom fusion | bytes 49152 | tf_op jit(solution)/shard_map/gather | solution.py:170
  1038.4 22.6 %scatter_custom_fusion.8 = f32[16384]{0:T(1024)} fusion(s32[4096]{0:T(1024)} %bitcast.902, f32[4096]{0:T(1024)S(1)} %fusion.83, f32[]{:T(128)} %constant.77.clone.1), kind=kCustom, calls=%fused_computation.425 | custom fusion | flops 4096 | bytes 66048 | tf_op jit(solution)/shard_map/scatter-add | solution.py:171
  1063.3 104.4 %all-reduce.23.cloned.1.call-done = f32[16384]{0:T(1024)} async-done(((f32[16384]{0:T(1024)}), f32[16384]{0:T(1024)}) %all-reduce.23.cloned.1.call-update) | async-done | bytes 65552
  (499 shorter events, 211.4 us)
Async XLA Ops:
  10.2 119.9 %all-to-all-start = ((f32[32,1,3]{2,1,0:T(1,128)}), f32[32,1,3]{2,1,0:T(1,128)S(1)}, u32[]{:S(2)}, u32[]{:S(2)}) async-start(f32[32,1,3]{2,1,0:T(1,128)} %bitcast.180), calls=%async_computation | async-start | bytes 32768 | tf_op jit(solution)/shard_map/all_to_all | solution.py:154
  20.3 192.4 %all-reduce.13.cloned.1.call-start = ((), (), s32[]{:S(2)}) async-start(), calls=%async_computation.3 | async-start | bytes 131072
  117.4 180.7 %collective-permute-start.1 = (f32[19,1,16,128]{3,2,1,0:T(8,128)}, f32[19,1,16,128]{3,2,1,0:T(8,128)}, u32[]{:S(2)}, u32[]{:S(2)}) collective-permute-start(f32[19,1,16,128]{3,2,1,0:T(8,128)} %get-tuple-element.159), channel_id=1, source_target_pairs={{8,0},{16,8},{24,16},{32,24},{40,32},{48,40},{56,48},{64,56},{72,6... | collective-permute-start | bytes 466952 | tf_op jit(solution)/shard_map/ppermute | solution.py:49
  123.8 173.2 %collective-permute-start = (f32[19,1,16,128]{3,2,1,0:T(8,128)S(1)}, f32[19,1,16,128]{3,2,1,0:T(8,128)}, u32[]{:S(2)}, u32[]{:S(2)}) collective-permute-start(f32[19,1,16,128]{3,2,1,0:T(8,128)S(1)} %get-tuple-element.160), channel_id=1, source_target_pairs={{0,8},{8,16},{16,24},{24,32},{32,40},{40,48},{48,56},{56,64},{64,7... | collective-permute-start | bytes 466952 | tf_op jit(solution)/shard_map/ppermute | solution.py:46
  131.6 15.1 %all-to-all-start.1 = ((f32[32,3,128]{2,1,0:T(4,128)}), f32[32,3,128]{2,1,0:T(4,128)S(1)}, u32[]{:S(2)}, u32[]{:S(2)}) async-start(f32[32,3,128]{2,1,0:T(4,128)} %reshape.2037), calls=%async_computation.1 | async-start | bytes 131072 | tf_op jit(solution)/shard_map/all_to_all | solution.py:147
  138.9 264.7 %all-reduce.15.cloned.1.call-start = ((), (), s32[]{:S(2)}) async-start(), calls=%async_computation.4 | async-start | bytes 131072
  297.0 297.6 %all-reduce.17.cloned.1.call-start = ((), (), s32[]{:S(2)}) async-start(), calls=%async_computation.5 | async-start | bytes 131072
  301.0 187.0 %collective-permute-start.3 = (f32[19,6,1,128]{3,2,1,0:T(1,128)S(1)}, f32[19,6,1,128]{3,2,1,0:T(1,128)S(1)}, u32[]{:S(2)}, u32[]{:S(2)}) collective-permute-start(f32[19,6,1,128]{3,2,1,0:T(1,128)S(1)} %get-tuple-element.100), channel_id=1, source_target_pairs={{1,0},{2,1},{3,2},{4,3},{5,4},{6,5},{7,6},{0,7},{9,8},{10,9},{11,1... | collective-permute-start | bytes 175112 | tf_op jit(solution)/shard_map/ppermute | solution.py:49
  303.0 184.9 %collective-permute-start.2 = (f32[19,6,1,128]{3,2,1,0:T(1,128)S(1)}, f32[19,6,1,128]{3,2,1,0:T(1,128)S(1)}, u32[]{:S(2)}, u32[]{:S(2)}) collective-permute-start(f32[19,6,1,128]{3,2,1,0:T(1,128)S(1)} %get-tuple-element.101), channel_id=1, source_target_pairs={{0,1},{1,2},{2,3},{3,4},{4,5},{5,6},{6,7},{7,0},{8,9},{9,10},{10,1... | collective-permute-start | bytes 175112 | tf_op jit(solution)/shard_map/ppermute | solution.py:46
  487.9 298.0 %all-reduce.19.cloned.1.call-start = ((), (), s32[]{:S(2)}) async-start(), calls=%async_computation.6 | async-start | bytes 131072
  679.2 297.5 %all-reduce.21.cloned.1.call-start = ((), (), s32[]{:S(2)}) async-start(), calls=%async_computation.7 | async-start | bytes 131072
  870.1 297.5 %all-reduce.23.cloned.1.call-start = ((), (), s32[]{:S(2)}) async-start(), calls=%async_computation.8 | async-start | bytes 131072
  870.2 190.9 %collective-permute-start.5 = (f32[19,1,16,128]{3,2,1,0:T(8,128)S(1)}, f32[19,1,16,128]{3,2,1,0:T(8,128)S(1)}, u32[]{:S(2)}, u32[]{:S(2)}) collective-permute-start(f32[19,1,16,128]{3,2,1,0:T(8,128)S(1)} %get-tuple-element.153), channel_id=1, source_target_pairs={{8,0},{16,8},{24,16},{32,24},{40,32},{48,40},{56,48},{64,56},{72,6... | collective-permute-start | bytes 466952 | tf_op jit(solution)/shard_map/ppermute | solution.py:49
  882.5 178.5 %collective-permute-start.4 = (f32[19,1,16,128]{3,2,1,0:T(8,128)S(1)}, f32[19,1,16,128]{3,2,1,0:T(8,128)S(1)}, u32[]{:S(2)}, u32[]{:S(2)}) collective-permute-start(f32[19,1,16,128]{3,2,1,0:T(8,128)S(1)} %get-tuple-element.154), channel_id=1, source_target_pairs={{0,8},{8,16},{16,24},{24,32},{32,40},{40,48},{48,56},{56,64},{64,7... | collective-permute-start | bytes 466952 | tf_op jit(solution)/shard_map/ppermute | solution.py:46
  1061.1 129.9 %collective-permute-start.7 = (f32[19,6,1,128]{3,2,1,0:T(1,128)S(1)}, f32[19,6,1,128]{3,2,1,0:T(1,128)S(1)}, u32[]{:S(2)}, u32[]{:S(2)}) collective-permute-start(f32[19,6,1,128]{3,2,1,0:T(1,128)S(1)} %get-tuple-element.98), channel_id=1, source_target_pairs={{1,0},{2,1},{3,2},{4,3},{5,4},{6,5},{7,6},{0,7},{9,8},{10,9},{11,1... | collective-permute-start | bytes 175112 | tf_op jit(solution)/shard_map/ppermute | solution.py:49
  1063.2 127.8 %collective-permute-start.6 = (f32[19,6,1,128]{3,2,1,0:T(1,128)S(1)}, f32[19,6,1,128]{3,2,1,0:T(1,128)S(1)}, u32[]{:S(2)}, u32[]{:S(2)}) collective-permute-start(f32[19,6,1,128]{3,2,1,0:T(1,128)S(1)} %get-tuple-element.99), channel_id=1, source_target_pairs={{0,1},{1,2},{2,3},{3,4},{4,5},{5,6},{6,7},{7,0},{8,9},{9,10},{10,1... | collective-permute-start | bytes 175112 | tf_op jit(solution)/shard_map/ppermute | solution.py:46
  1170.3 18.1 %all-to-all-start.2 = ((f32[32,1,3]{2,1,0:T(1,128)}), f32[32,1,3]{2,1,0:T(1,128)S(1)}, u32[]{:S(2)}, u32[]{:S(2)}) async-start(f32[32,1,3]{2,1,0:T(1,128)} %bitcast.199), calls=%async_computation.2 | async-start | bytes 32768 | tf_op jit(solution)/shard_map/all_to_all | solution.py:177
  1202.4 12.4 collective-permute-start.11
  1205.1 9.7 collective-permute-start.10
  1229.2 10.1 collective-permute-start.15
  1229.5 9.8 collective-permute-start.14
  1255.7 9.2 collective-permute-start.19
  1255.8 9.1 collective-permute-start.18
  1279.1 9.2 collective-permute-start.23
  (46 other events, 742.3 us)
Sparse Core Ops, SparseCore 0:
  106.2 106.4 all-reduce.12
  297.1 106.4 all-reduce.14
  488.0 106.5 all-reduce.16
  679.3 106.4 all-reduce.18
  870.2 106.4 all-reduce.20
  1061.1 106.4 all-reduce.22
where the time goes:
time: 1310 us; the launch traced here: 1300 us
  waiting for transfers between devices  631 us (48%)
  blocking collectives  226 us (17%)
  local copies, waits for them, and re-layouts  170 us (13%)
  other arithmetic  156 us (12%)
  starting transfers between devices  80.7 us (6%)
  matrix products  17.4 us (1%)
  between operations  17.1 us (1%)
    unnamed x12, waiting for transfers between devices  570 us
    all_gather x6, blocking collectives, local(): group_pressure = lax.all_gather(pressure, 'sub', axis=0, tiled=True)  226 us
    gather x12, local copies, waits for them, and re-layouts, local(): flows = junction_flows(matrix, live, group_pressure[links])  138 us
    scatter-add x6, other arithmetic, local(): jax.ops.segment_sum(-flows.reshape(-1), links.reshape(-1), num_segments=g...  136 us
    ppermute x12, starting transfers between devices, extended(): lax.ppermute(lax.slice_in_dim(block, 0, width, axis=dim), axis, backward)  44.9 us
    ppermute x12, waiting for transfers between devices, extended(): lax.ppermute(lax.slice_in_dim(block, block.shape[dim] - width, None, axis...  40.5 us
  transfers between devices with their start and end apart: 33, of which 20 were waited for; matrix products, arithmetic and copies ran while one was open for 17% of the time, Pallas kernels for 0%

commit v1 on v0

v1 whole, which is shorter than its diff:
```python
import functools

import jax
import jax.numpy as jnp
import numpy as np
from jax import lax
from jax.experimental import pallas as pl
from jax.experimental.pallas import tpu as pltpu
from jax.sharding import PartitionSpec as P

STEPS = 6
SLOTS = 3
MESH = pl.DeviceIdType.MESH
F32 = jnp.float32
BF16 = jnp.bfloat16
HIGHEST = lax.Precision.HIGHEST

VELOCITIES = [
    (0, 0, 0),
    (1, 0, 0),
    (-1, 0, 0),
    (0, 1, 0),
    (0, -1, 0),
    (0, 0, 1),
    (0, 0, -1),
    (1, 1, 0),
    (-1, -1, 0),
    (1, -1, 0),
    (-1, 1, 0),
    (1, 0, 1),
    (-1, 0, -1),
    (1, 0, -1),
    (-1, 0, 1),
    (0, 1, 1),
    (0, -1, -1),
    (0, 1, -1),
    (0, -1, 1),
]
OPPOSITE = [0, 2, 1, 4, 3, 6, 5, 8, 7, 10, 9, 12, 11, 14, 13, 16, 15, 18, 17]
RELAXATION = 1.25
DENSITY_SCALE = 0.1
X_UP = [i for i, c in enumerate(VELOCITIES) if c[0] == 1]
X_DOWN = [i for i, c in enumerate(VELOCITIES) if c[0] == -1]
Y_UP = [i for i, c in enumerate(VELOCITIES) if c[1] == 1]
Y_DOWN = [i for i, c in enumerate(VELOCITIES) if c[1] == -1]
CORNERS = [(7, 1, 1), (8, -1, -1), (9, 1, -1), (10, -1, 1)]


def iota(shape, axis):
    return lax.broadcasted_iota(jnp.int32, shape, axis)


def collide_sites(h, solid, mask, imposed):
    w0, w1, w2 = 1.0 / 3.0, 1.0 / 18.0, 1.0 / 36.0
    plus = {i: h[i] + h[i + 1] for i in range(1, 19, 2)}
    minus = {i: h[i] - h[i + 1] for i in range(1, 19, 2)}
    near = plus[1] + plus[3] + plus[5]
    far = (plus[7] + plus[9]) + (plus[11] + plus[13]) + (plus[15] + plus[17])
    density = 1.0 + (w0 * h[0] + w1 * near + w2 * far)
    inverse = 1.0 / density
    ux = (w1 * minus[1] + w2 * ((minus[7] + minus[9]) + (minus[11] + minus[13]))) * inverse
    uy = (w1 * minus[3] + w2 * ((minus[7] - minus[9]) + (minus[15] + minus[17]))) * inverse
    uz = (w1 * minus[5] + w2 * ((minus[11] - minus[13]) + (minus[15] - minus[17]))) * inverse
    base = 1.0 - 1.5 * (ux * ux + uy * uy + uz * uz)
    along = {1: ux, 3: uy, 5: uz, 7: ux + uy, 9: ux - uy, 11: ux + uz, 13: ux - uz, 15: uy + uz, 17: uy - uz}
    scale = jnp.where(mask, imposed, RELAXATION * density)
    shift = jnp.where(mask, -1.0, -RELAXATION)
    keep = jnp.where(mask, 0.0, 1.0 - RELAXATION)
    bounce = jnp.logical_and(solid, jnp.logical_not(mask))
    post = [None] * 19
    post[0] = jnp.where(bounce, h[0], scale * base + (shift + keep * h[0]))
    for i in range(1, 19, 2):
        c = along[i]
        even = base + 4.5 * (c * c)
        odd = 3.0 * c
        post[i] = jnp.where(bounce, h[i + 1], scale * (even + odd) + (shift + keep * h[i]))
        post[i + 1] = jnp.where(bounce, h[i], scale * (even - odd) + (shift + keep * h[i + 1]))
    return post


def off_diagonals(live, res, cross):
    rows = [[None] * 4 for _ in range(4)]
    sides = [[None] * 4 for _ in range(4)]
    zero = jnp.zeros_like(live[0])
    for k in range(4):
        for l in range(4):
            if k == l:
                rows[k][l] = res[k]
                sides[k][l] = live[k]
            else:
                rows[k][l] = live[k] * live[l] * (0.5 * (cross[k][l] + cross[l][k]))
                sides[k][l] = zero
    for c in range(4):
        inverse = 1.0 / rows[c][c]
        for r in range(c + 1, 4):
            factor = rows[r][c] * inverse
            for l in range(c + 1, 4):
                rows[r][l] = rows[r][l] - factor * rows[c][l]
            for l in range(c + 1):
                sides[r][l] = sides[r][l] - factor * sides[c][l]
    answer = [None] * 4
    for r in reversed(range(4)):
        inverse = 1.0 / rows[r][r]
        answer[r] = []
        for l in range(4):
            running = sides[r][l]
            for c in range(r + 1, 4):
                running = running - rows[r][c] * answer[c][l]
            answer[r].append(running * inverse)
    ones = [answer[k][0] + answer[k][1] + answer[k][2] + answer[k][3] for k in range(4)]
    total = 1.0 / (live[0] * ones[0] + live[1] * ones[1] + live[2] * ones[2] + live[3] * ones[3])
    pairs = []
    for a in range(4):
        for b in range(a + 1, 4):
            pairs.append(live[a] * live[b] * (answer[a][b] - ones[a] * ones[b] * total))
    return pairs


def split2(x):
    high = x.astype(BF16)
    return high, (x - high.astype(F32)).astype(BF16)


def kernel(
    nb,
    ns,
    pop_ref,
    solid_ref,
    bp_ref,
    col_ref,
    dest_ref,
    seg_ref,
    segp_ref,
    rate_ref,
    leak_ref,
    w_ref,
    mem_ref,
    arity_ref,
    res_ref,
    cross_ref,
    pop_out,
    seg_out,
    bp_out,
    post,
    mask_ref,
    imposed_ref,
    sxu,
    sxd,
    syu,
    syd,
    sc,
    rxu,
    rxd,
    ryu,
    ryd,
    rc,
    ptab,
    rate2,
    leak2,
    inflow2,
    flow,
    other_mem,
    gbuf,
    row_at,
    oh_c,
    oh_r,
    part,
    rs,
    msg,
    arrived,
    pick,
    ids_ref,
    ret_out,
    ret_in,
    halo_s,
    halo_r,
    first_s,
    first_r,
    pair_s,
    pair_r,
    rs_s,
    rs_r,
    ag_s,
    ag_r,
    msg_s,
    msg_r,
    ret_s,
    ret_r,
):
    ny = ns // 2
    rows = segp_ref.shape[0]
    junctions = mem_ref.shape[1]
    links = 4 * junctions
    blocks = col_ref.shape[1]
    cells_x, cells_y, cells_z = solid_ref.shape
    b, s = lax.axis_index("brick"), lax.axis_index("sub")
    hi, y = s // ny, lax.rem(s, ny)
    other = 1 - hi
    partner = (b, other * ny + y)

    def at(db, ds):
        return (lax.rem(b + db + nb, nb), lax.rem(s + ds + ns, ns))

    def ring(k):
        return (b, hi * ny + lax.rem(y + k, ny))

    def copy(src, dst, send, recv, device):
        return pltpu.make_async_remote_copy(
            src_ref=src, dst_ref=dst, send_sem=send, recv_sem=recv, device_id=device, device_id_type=MESH
        )

    barrier = pltpu.get_barrier_semaphore()

    def greet(k, carry):
        pl.semaphore_signal(barrier, inc=1, device_id=at(k, 0), device_id_type=MESH)
        return carry

    lax.fori_loop(1, nb, greet, 0)
    for k in range(1, ns):
        pl.semaphore_signal(barrier, inc=1, device_id=at(0, k), device_id_type=MESH)
    for _, cx, cy in CORNERS:
        pl.semaphore_signal(barrier, inc=1, device_id=at(cx, cy), device_id_type=MESH)

    dest = dest_ref[...]
    eye = iota((blocks, blocks), 0) == iota((blocks, blocks), 1)
    dest_column = jnp.sum(jnp.where(eye, dest, 0), axis=1, keepdims=True)
    earlier = jnp.logical_and(dest_column == dest, iota((blocks, blocks), 0) < iota((blocks, blocks), 1))
    slot = jnp.sum(jnp.where(earlier, 1, 0), axis=0, keepdims=True)
    r = iota((nb * 8, blocks), 0)
    chosen = jnp.logical_and((r >> 3) == dest, (r & 3) == slot)
    pick[...] = jnp.where(chosen, 1.0, 0.0)
    columns = cells_x * cells_y
    hits = iota((columns, blocks), 0) == col_ref[...]
    selector = lax.dot_general(
        jnp.where(chosen, 1.0, 0.0).astype(BF16),
        jnp.where(hits, 1.0, 0.0).astype(BF16),
        (((1,), (1,)), ((), ())),
        preferred_element_type=F32,
    )
    axial = jnp.zeros((columns, cells_z), F32)
    for i, c in enumerate(VELOCITIES):
        if c[0]:
            weight = c[0] * (1.0 / 18.0 if i < 7 else 1.0 / 36.0)
            axial = axial + weight * pop_ref[i].reshape(columns, cells_z)
    profiles = jnp.dot(selector, axial, precision=HIGHEST, preferred_element_type=F32)
    numbers = jnp.sum(jnp.where(chosen, seg_ref[...] + 1, 0), axis=1, keepdims=True) - 1
    numbers = jnp.broadcast_to(numbers.astype(F32), (nb * 8, cells_z))
    is_label = (iota((nb * 8, cells_z), 0) & 4) != 0
    msg[...] = jnp.where(is_label, numbers, profiles).reshape(nb, 8, cells_z)

    found = jnp.sum(jnp.where(hits, 1.0, 0.0), axis=1, keepdims=True)
    pressed = jnp.sum(jnp.where(hits, bp_ref[...], 0.0), axis=1, keepdims=True)
    mask_ref[...] = jnp.broadcast_to(found, (columns, cells_z)).reshape(cells_x, cells_y, cells_z)
    imposed_ref[...] = jnp.broadcast_to(1.0 + DENSITY_SCALE * pressed, (columns, cells_z)).reshape(
        cells_x, cells_y, cells_z
    )

    live = [jnp.where(arity_ref[...] > k, 1.0, 0.0) for k in range(4)]
    pairs = off_diagonals(
        live,
        [res_ref[k : k + 1, :] for k in range(4)],
        [[cross_ref[k, l : l + 1, :] for l in range(4)] for k in range(4)],
    )
    for n, value in enumerate(pairs):
        gbuf[0, n : n + 1, :] = value
    gbuf[0, 6:8, :] = jnp.zeros((2, junctions), F32)

    ptab[y, hi] = segp_ref[...]
    rate2[hi] = rate_ref[...]
    leak2[hi] = leak_ref[...]

    pl.semaphore_wait(barrier, nb - 1 + ns - 1 + len(CORNERS))

    first = [
        copy(segp_ref, ptab.at[y, hi], first_s.at[k - 1], first_r.at[k - 1], at(0, k)) for k in range(1, ns)
    ]
    for c in first:
        c.start()
    pair = [
        copy(mem_ref, other_mem, pair_s.at[0], pair_r.at[0], partner),
        copy(gbuf.at[0], gbuf.at[1], pair_s.at[1], pair_r.at[1], partner),
        copy(rate_ref, rate2.at[hi], pair_s.at[2], pair_r.at[2], partner),
        copy(leak_ref, leak2.at[hi], pair_s.at[3], pair_r.at[3], partner),
    ]
    for c in pair:
        c.start()
    pair_inflow = copy(flow, inflow2.at[hi], pair_s.at[4], pair_r.at[4], partner)

    def message(k):
        target = lax.rem(b + k, nb)
        return copy(msg.at[target], arrived.at[b], msg_s.at[k - 1], msg_r.at[k - 1], (target, s))

    def answer(k):
        target = lax.rem(b + k, nb)
        return copy(ret_out.at[target], ret_in.at[b], ret_s.at[k - 1], ret_r.at[k - 1], (target, s))

    def start_message(k, carry):
        message(k).start()
        return carry

    lax.fori_loop(1, nb, start_message, 0)
    arrived[b] = msg[b]

    def halo(parity):
        copies = [
            (sxu, rxu, (1, 0)),
            (sxd, rxd, (-1, 0)),
            (syu, ryu, (0, 1)),
            (syd, ryd, (0, -1)),
        ]
        out = [
            copy(src, dst.at[parity], halo_s.at[n], halo_r.at[parity, n], at(*to))
            for n, (src, dst, to) in enumerate(copies)
        ]
        for n, (_, cx, cy) in enumerate(CORNERS):
            out.append(
                copy(sc.at[n], rc.at[parity, n], halo_s.at[4 + n], halo_r.at[parity, 4 + n], at(cx, cy))
            )
        return out

    halves = cells_y // 8

    def collide(source):
        def tile(n, carry):
            x, first_row = n // halves, pl.multiple_of(lax.rem(n, halves) * 8, 8)
            span = pl.ds(first_row, 8)
            h = [source[i, x, span, :] for i in range(19)]
            out = collide_sites(
                h, solid_ref[x, span, :] > 0, mask_ref[x, span, :] > 0.5, imposed_ref[x, span, :]
            )
            for i in range(19):
                post[i, x, span, :] = out[i]
            return carry

        lax.fori_loop(0, cells_x * halves, tile, 0)

    def pack():
        for n, i in enumerate(X_UP):
            sxu[n] = post[i, cells_x - 1]
        for n, i in enumerate(X_DOWN):
            sxd[n] = post[i, 0]
        for n, i in enumerate(Y_UP):
            for x in range(cells_x):
                syu[n, x : x + 1, :] = post[i, x, cells_y - 1 : cells_y, :]
        for n, i in enumerate(Y_DOWN):
            for x in range(cells_x):
                syd[n, x : x + 1, :] = post[i, x, 0:1, :]
        for n, (i, cx, cy) in enumerate(CORNERS):
            x = cells_x - 1 if cx > 0 else 0
            row = cells_y - 1 if cy > 0 else 0
            sc[n] = jnp.broadcast_to(post[i, x, row : row + 1, :], (8, cells_z))

    def stream(parity):
        edge = iota((cells_y, cells_z), 0)
        for i, (cx, cy, cz) in enumerate(VELOCITIES):
            for x in range(cells_x):
                xs = x - cx
                inside = 0 <= xs < cells_x
                if inside:
                    value = post[i, xs]
                elif cx > 0:
                    value = rxu[parity, X_UP.index(i)]
                else:
                    value = rxd[parity, X_DOWN.index(i)]
                if cy:
                    if not inside:
                        n = [c[0] for c in CORNERS].index(i)
                        row = rc[parity, n, 0:1, :]
                    elif cy > 0:
                        row = ryu[parity, Y_UP.index(i), xs : xs + 1, :]
                    else:
                        row = ryd[parity, Y_DOWN.index(i), xs : xs + 1, :]
                    value = pltpu.roll(value, cy % cells_y, 0)
                    value = jnp.where(edge == (0 if cy > 0 else cells_y - 1), row, value)
                if cz:
                    value = pltpu.roll(value, cz % cells_z, 1)
                pop_out[i, x] = value

    collide(pop_ref)
    pack()
    for c in halo(0):
        c.start()

    def build(n, ref):
        m = jnp.concatenate([ref[k : k + 1, :] for k in range(4)], axis=1)
        per = rows * 128
        sub = m // per
        row = (lax.rem(sub, ny) * 2 + sub // ny) * rows + (lax.rem(m, per) >> 7)
        row_at[n] = row
        lines = iota((128, links), 0)
        oh_c[n] = jnp.where(lines == (m & 127), 1.0, 0.0).astype(BF16)
        oh_r[n] = jnp.where(iota((ns * rows, links), 0) == row, 1.0, 0.0).astype(BF16)

    build(0, mem_ref)
    pair[0].wait()
    build(1, other_mem)
    for c in pair[1:]:
        c.wait()
    for c in first:
        c.wait()

    def flows(n, table):
        members = oh_c[n]
        found = jnp.dot(table, jnp.concatenate([members, members], axis=0), preferred_element_type=F32)
        q = jnp.sum(jnp.where(iota((ns * rows, links), 0) == row_at[n], found, 0.0), axis=0, keepdims=True)
        q = [q[:, k * junctions : (k + 1) * junctions] for k in range(4)]
        f = [None] * 4
        count = 0
        for k in range(4):
            for l in range(k + 1, 4):
                term = gbuf[n, count : count + 1, :] * (q[l] - q[k])
                f[k] = term if f[k] is None else f[k] + term
                f[l] = -term if f[l] is None else f[l] - term
                count += 1
        high, low = split2(jnp.concatenate(f, axis=1))
        return lax.dot_general(
            oh_r[n],
            jnp.concatenate([members * high, members * low], axis=0),
            (((1,), (1,)), ((), ())),
            preferred_element_type=F32,
        )

    def inflows():
        def wait_message(k, carry):
            message(k).wait()
            return carry

        lax.fori_loop(1, nb, wait_message, 0)
        got = arrived[...].reshape(nb * 8, cells_z)
        numbers = pltpu.roll(got, nb * 8 - 4, 0)
        at_row = iota((nb * 8, cells_z), 0)
        holds = jnp.logical_and((at_row & 4) == 0, (at_row & 3) < SLOTS)
        numbers = jnp.where(holds, numbers.astype(jnp.int32), -1)
        ids_ref[...] = numbers
        lane = iota((nb * 8, 128), 1)

        def chunk(n, carry):
            weights = w_ref[pl.ds(pl.multiple_of(n * 128, 128), 128), :]
            value = lax.dot_general(
                got, weights, (((1,), (1,)), ((), ())), precision=HIGHEST, preferred_element_type=F32
            )
            value = jnp.where(numbers == lane + n * 128, value, 0.0)
            flow[pl.ds(n, 1), :] = jnp.sum(value, axis=0, keepdims=True)
            return carry

        lax.fori_loop(0, rows, chunk, 0)
        pair_inflow.start()
        inflow2[hi] = flow[...]
        pair_inflow.wait()

    def step(t, carry):
        parity = lax.rem(t, 2)
        table = jnp.concatenate(split2(ptab[...].reshape(ns * rows, 128)), axis=1)
        both = flows(0, table) + flows(1, table)
        part[...] = (both[:, :128] + both[:, 128:]).reshape(ny, 2, rows, 128)
        scatter = [
            copy(part.at[lax.rem(y + k, ny)], rs.at[k - 1], rs_s.at[k - 1], rs_r.at[k - 1], ring(k))
            for k in range(1, ny)
        ]
        for c in scatter:
            c.start()

        now = halo(parity)
        for c in now:
            c.wait_recv()
        stream(parity)
        for c in now:
            c.wait_send()

        @pl.when(t < STEPS - 1)
        def _():
            collide(pop_out)
            pack()
            for c in halo(1 - parity):
                c.start()

        @pl.when(t == 0)
        def _():
            inflows()

        for c in scatter:
            c.wait()
        balance = part[y]
        for k in range(1, ny):
            balance = balance + rs[k - 1]
        p = ptab[y]
        ptab[y] = p + rate2[...] * (inflow2[...] - balance - leak2[...] * p)

        @pl.when(t < STEPS - 1)
        def _():
            gather = [
                copy(ptab.at[y], ptab.at[y], ag_s.at[k - 1], ag_r.at[k - 1], ring(k)) for k in range(1, ny)
            ]
            for c in gather:
                c.start()
            for c in gather:
                c.wait()

        return carry

    lax.fori_loop(0, STEPS, step, 0)
    final = ptab[y, hi]
    seg_out[...] = final

    numbers = ids_ref[...]
    lane = iota((nb * 8, 128), 1)
    value = jnp.zeros((nb * 8, 128), F32)
    for n in range(rows):
        value = value + jnp.where(numbers == lane + n * 128, final[n : n + 1, :], 0.0)
    value = jnp.sum(value, axis=1, keepdims=True)
    ret_out[...] = jnp.broadcast_to(value, (nb * 8, 128)).reshape(nb, 8, 128)

    def start_answer(k, carry):
        answer(k).start()
        return carry

    def wait_answer(k, carry):
        answer(k).wait()
        return carry

    lax.fori_loop(1, nb, start_answer, 0)
    ret_in[b] = ret_out[b]
    lax.fori_loop(1, nb, wait_answer, 0)
    back = ret_in[...].reshape(nb * 8, 128)[:, :blocks]
    is_value = (iota((nb * 8, blocks), 0) & 4) == 0
    bp_out[...] = jnp.sum(
        jnp.where(jnp.logical_and(is_value, pick[...] > 0.5), back, 0.0), axis=0, keepdims=True
    )


def local(
    populations,
    solid,
    boundary_pressure,
    block_col,
    block_dest,
    block_seg,
    seg_pressure,
    seg_rate,
    seg_leak,
    profile_weights,
    junc_members,
    junc_arity,
    junc_res,
    junc_cross,
):
    nb, ns = lax.axis_size("brick"), lax.axis_size("sub")
    ny = ns // 2
    _, cx, cy, cz = populations.shape
    segs, blocks, junctions = seg_pressure.shape[0], block_col.shape[0], junc_arity.shape[0]
    rows, links = segs // 128, 4 * junctions
    vmem, dma = pltpu.VMEM, pltpu.SemaphoreType.DMA
    scratch = [
        vmem((19, cx, cy, cz), F32),
        vmem((cx, cy, cz), F32),
        vmem((cx, cy, cz), F32),
        vmem((5, cy, cz), F32),
        vmem((5, cy, cz), F32),
        vmem((5, cx, cz), F32),
        vmem((5, cx, cz), F32),
        vmem((4, 8, cz), F32),
        vmem((2, 5, cy, cz), F32),
        vmem((2, 5, cy, cz), F32),
        vmem((2, 5, cx, cz), F32),
        vmem((2, 5, cx, cz), F32),
        vmem((2, 4, 8, cz), F32),
        vmem((ny, 2, rows, 128), F32),
        vmem((2, rows, 128), F32),
        vmem((2, rows, 128), F32),
        vmem((2, rows, 128), F32),
        vmem((rows, 128), F32),
        vmem((4, junctions), jnp.int32),
        vmem((2, 8, junctions), F32),
        vmem((2, 1, links), jnp.int32),
        vmem((2, 128, links), BF16),
        vmem((2, ns * rows, links), BF16),
        vmem((ny, 2, rows, 128), F32),
        vmem((ny - 1, 2, rows, 128), F32),
        vmem((nb, 8, cz), F32),
        vmem((nb, 8, cz), F32),
        vmem((nb * 8, blocks), F32),
        vmem((nb * 8, cz), jnp.int32),
        vmem((nb, 8, 128), F32),
        vmem((nb, 8, 128), F32),
        dma((8,)),
        dma((2, 8)),
        dma((ns - 1,)),
        dma((ns - 1,)),
        dma((5,)),
        dma((5,)),
        dma((ny - 1,)),
        dma((ny - 1,)),
        dma((ny - 1,)),
        dma((ny - 1,)),
        dma((nb - 1,)),
        dma((nb - 1,)),
        dma((nb - 1,)),
        dma((nb - 1,)),
    ]
    spec = pl.BlockSpec(memory_space=vmem)
    lattice, pressure, back = pl.pallas_call(
        functools.partial(kernel, nb, ns),
        out_shape=(
            jax.ShapeDtypeStruct(populations.shape, F32),
            jax.ShapeDtypeStruct((rows, 128), F32),
            jax.ShapeDtypeStruct((1, blocks), F32),
        ),
        in_specs=[spec] * 14,
        out_specs=(spec, spec, spec),
        scratch_shapes=scratch,
        compiler_params=pltpu.CompilerParams(
            collective_id=0, has_side_effects=True, vmem_limit_bytes=48 * 2**20
        ),
        name="coupled",
    )(
        populations,
        solid,
        boundary_pressure.reshape(1, blocks),
        block_col.reshape(1, blocks),
        block_dest.reshape(1, blocks),
        block_seg.reshape(1, blocks),
        seg_pressure.reshape(rows, 128),
        seg_rate.reshape(rows, 128),
        seg_leak.reshape(rows, 128),
        profile_weights,
        junc_members,
        junc_arity.reshape(1, junctions),
        junc_res,
        junc_cross,
    )
    return lattice, pressure.reshape(segs), back.reshape(blocks)


def solution(mesh):
    return jax.shard_map(
        local,
        mesh=mesh,
        in_specs=(
            P(None, "brick", "sub", None),
            P("brick", "sub", None),
            P(("brick", "sub")),
            P(("brick", "sub")),
            P(("brick", "sub"), None),
            P(("brick", "sub")),
            P(("brick", "sub")),
            P(("brick", "sub")),
            P(("brick", "sub")),
            P(("brick", "sub"), None),
            P(None, ("brick", "sub")),
            P(("brick", "sub")),
            P(None, ("brick", "sub")),
            P(None, None, ("brick", "sub")),
        ),
        out_specs=(P(None, "brick", "sub", None), P(("brick", "sub")), P(("brick", "sub"))),
        check_vma=False,
    )
```

time: 1310 us -> 101 us (0.08)
  waiting for transfers between devices: 631 us -> 0 us
  blocking collectives: 226 us -> 0 us
  local copies, waits for them, and re-layouts: 170 us -> 9.35 us
  other arithmetic: 156 us -> 0 us
  Pallas kernels: 0 us -> 90.4 us
  starting transfers between devices: 80.7 us -> 0 us
  matrix products: 17.4 us -> 0 us
  between operations: 17.1 us -> 0.7 us
    unnamed x12 -> x0, waiting for transfers between devices: 570 us -> none
    all_gather x6 -> x0, blocking collectives: 226 us -> none  [local(): group_pressure = lax.all_gather(pressure, 'sub', axis=0, tiled=True)]
    gather x23 -> x0, local copies, waits for them, and re-layouts: 145 us -> none  [the longest x12 138 us: local(): flows = junction_flows(matrix, live, group_pressure[links])]
    scatter-add x7 -> x0, other arithmetic: 137 us -> none  [the longest x6 136 us: local(): jax.ops.segment_sum(-flows.reshape(-1), links.reshape(-1), num_segments=g...]
    pallas_call x0 -> x1, Pallas kernels: none -> 90.4 us  [local(): pl.pallas_call(functools.partial(kernel, nb, ns), out_shape=(jax.ShapeDty...]
    ppermute x24 -> x0, starting transfers between devices: 52 us -> none  [the longest x12 44.9 us: extended(): lax.ppermute(lax.slice_in_dim(block, 0, width, axis=dim), axis, backward)]
    ppermute x24 -> x0, waiting for transfers between devices: 47.5 us -> none  [the longest x12 40.5 us: extended(): lax.ppermute(lax.slice_in_dim(block, block.shape[dim] - width, None, axis...]
    all_to_all x3 -> x0, starting transfers between devices: 28.5 us -> none  [the longest x1 11.1 us: local(): lax.all_to_all(answer_back, 'brick', split_axis=0, concat_axis=0, tiled=T...]
  transfers between devices with their start and end apart: 33 -> 0, of which waited for: 20 -> 0; matrix products, arithmetic and copies ran while one was open for 17% -> 0% of each run, Pallas kernels for 0% -> 0%
where the time goes in v1:
time: 101 us; the launch traced here: 100 us
  Pallas kernels  90.4 us (90%)
  local copies, waits for them, and re-layouts  9.35 us (9%)
    pallas_call x1, Pallas kernels, local(): pl.pallas_call(functools.partial(kernel, nb, ns), out_shape=(jax.ShapeDty...  90.4 us
    unnamed x31, local copies, waits for them, and re-layouts  9.35 us

profile of v1, /device:TPU:1, one launch (start us, length us, event | category | flops | bytes accessed | tf_op | source)
XLA Modules:
  0.0 100.5 jit_solution(2029182331184480860)
XLA Ops:
  0.6 0.0 copy-start.6
  0.6 0.0 copy-start.9
  0.7 0.0 copy-start.13
  0.7 0.0 copy-start.10
  0.7 0.0 copy-start.11
  0.7 0.0 copy-start.12
  0.7 0.6 copy-done.6
  1.3 0.0 copy-done.9
  1.3 0.0 copy-done.13
  1.3 0.0 copy-done.10
  1.3 0.0 copy-done.11
  1.4 0.0 copy-done.12
  1.4 1.2 %copy-done = f32[2048,128]{1,0:T(8,128)S(1)} copy-done((f32[2048,128]{1,0:T(8,128)S(1)}, f32[2048,128]{1,0:T(8,128)}, u32[]{:S(2)}) %copy-start) | copy-done | bytes 1048600
  2.6 1.1 %copy-done.1 = f32[19,4,16,128]{3,2,1,0:T(8,128)S(1)} copy-done((f32[19,4,16,128]{3,2,1,0:T(8,128)S(1)}, f32[19,4,16,128]{3,2,1,0:T(8,128)}, u32[]{:S(2)}) %copy-start.1) | copy-done | bytes 622616
  3.7 0.8 copy-done.2
  4.5 0.8 copy-done.3
  5.3 0.7 copy-done.4
  6.0 0.7 copy-done.5
  6.7 0.7 copy-done.7
  7.4 0.7 copy-done.8
  8.1 90.4 %coupled.1 = (f32[19,4,16,128]{3,2,1,0:T(8,128)S(1)}, f32[16,128]{1,0:T(8,128)S(1)}, f32[1,32]{1,0:T(1,128)S(1)}) custom-call(f32[19,4,16,128]{3,2,1,0:T(8,128)S(1)} %copy-done.1, s32[4,16,128]{2,1,0:T(8,128)S(1)} %copy-done.3, f32[1,32]{1,0:T(1,128)S(1)} %bitcast.15, s32[1,32]{1,0:T(1,128)S(1)} %bitcast.16, s32[1,32]{1,0:T(1,128)S(1)} %bitcast.17, ...), custom_call_target="tpu_custom_call" | custom-call | tf_op jit(solution)/shard_map/coupled/pallas_call | solution.py:601
  98.5 0.8 copy.20
  99.4 0.6 copy.21
  100.0 0.5 copy.22
  (8 shorter events, 0.0 us)
Async XLA Ops:
  0.6 0.7 copy-start.6
  0.6 0.7 copy-start.9
  0.7 0.7 copy-start.13
  0.7 0.7 copy-start.10
  0.7 0.7 copy-start.11
  0.7 0.7 copy-start.12
  1.4 1.2 %copy-start = (f32[2048,128]{1,0:T(8,128)S(1)}, f32[2048,128]{1,0:T(8,128)}, u32[]{:S(2)}) copy-start(f32[2048,128]{1,0:T(8,128)} %w_ref.1) | copy-start | bytes 3145732
  2.6 1.1 %copy-start.1 = (f32[19,4,16,128]{3,2,1,0:T(8,128)S(1)}, f32[19,4,16,128]{3,2,1,0:T(8,128)}, u32[]{:S(2)}) copy-start(f32[19,4,16,128]{3,2,1,0:T(8,128)} %pop_ref.1) | copy-start | bytes 1867780
  3.7 0.8 copy-start.2
  4.5 0.8 copy-start.3
  5.3 0.7 copy-start.4
  6.0 0.7 copy-start.5
  6.7 0.7 copy-start.7
  7.4 0.7 copy-start.8

commit v2 on v1

--- a/solution.py
+++ b/solution.py
@@ -121,9 +121,33 @@
     return high, (x - high.astype(F32)).astype(BF16)
 
 
+def split3(x):
+    high = x.astype(BF16)
+    rest = x - high.astype(F32)
+    middle = rest.astype(BF16)
+    return high, middle, (rest - middle.astype(F32)).astype(BF16)
+
+
 def kernel(
     nb,
     ns,
+    pop_hbm,
+    solid_hbm,
+    bp_hbm,
+    col_hbm,
+    dest_hbm,
+    seg_hbm,
+    segp_hbm,
+    rate_hbm,
+    leak_hbm,
+    w_hbm,
+    mem_hbm,
+    arity_hbm,
+    res_hbm,
+    cross_hbm,
+    pop_out,
+    seg_out,
+    bp_out,
     pop_ref,
     solid_ref,
     bp_ref,
@@ -131,16 +155,12 @@
     dest_ref,
     seg_ref,
     segp_ref,
-    rate_ref,
-    leak_ref,
     w_ref,
     mem_ref,
     arity_ref,
     res_ref,
     cross_ref,
-    pop_out,
-    seg_out,
-    bp_out,
+    load_s,
     post,
     mask_ref,
     imposed_ref,
@@ -155,9 +175,9 @@
     ryd,
     rc,
     ptab,
-    rate2,
-    leak2,
-    inflow2,
+    stage,
+    rates,
+    inflow_all,
     flow,
     other_mem,
     gbuf,
@@ -165,23 +185,25 @@
     oh_c,
     oh_r,
     part,
-    rs,
     msg,
     arrived,
     pick,
     ids_ref,
+    w_parts,
     ret_out,
     ret_in,
     halo_s,
     halo_r,
     first_s,
     first_r,
+    rates_s,
+    rates_r,
+    inflow_s,
+    inflow_r,
     pair_s,
     pair_r,
-    rs_s,
-    rs_r,
-    ag_s,
-    ag_r,
+    part_s,
+    part_r,
     msg_s,
     msg_r,
     ret_s,
@@ -221,40 +243,32 @@
     for _, cx, cy in CORNERS:
         pl.semaphore_signal(barrier, inc=1, device_id=at(cx, cy), device_id_type=MESH)
 
-    dest = dest_ref[...]
-    eye = iota((blocks, blocks), 0) == iota((blocks, blocks), 1)
-    dest_column = jnp.sum(jnp.where(eye, dest, 0), axis=1, keepdims=True)
-    earlier = jnp.logical_and(dest_column == dest, iota((blocks, blocks), 0) < iota((blocks, blocks), 1))
-    slot = jnp.sum(jnp.where(earlier, 1, 0), axis=0, keepdims=True)
-    r = iota((nb * 8, blocks), 0)
-    chosen = jnp.logical_and((r >> 3) == dest, (r & 3) == slot)
-    pick[...] = jnp.where(chosen, 1.0, 0.0)
-    columns = cells_x * cells_y
-    hits = iota((columns, blocks), 0) == col_ref[...]
-    selector = lax.dot_general(
-        jnp.where(chosen, 1.0, 0.0).astype(BF16),
-        jnp.where(hits, 1.0, 0.0).astype(BF16),
-        (((1,), (1,)), ((), ())),
-        preferred_element_type=F32,
-    )
-    axial = jnp.zeros((columns, cells_z), F32)
-    for i, c in enumerate(VELOCITIES):
-        if c[0]:
-            weight = c[0] * (1.0 / 18.0 if i < 7 else 1.0 / 36.0)
-            axial = axial + weight * pop_ref[i].reshape(columns, cells_z)
-    profiles = jnp.dot(selector, axial, precision=HIGHEST, preferred_element_type=F32)
-    numbers = jnp.sum(jnp.where(chosen, seg_ref[...] + 1, 0), axis=1, keepdims=True) - 1
-    numbers = jnp.broadcast_to(numbers.astype(F32), (nb * 8, cells_z))
-    is_label = (iota((nb * 8, cells_z), 0) & 4) != 0
-    msg[...] = jnp.where(is_label, numbers, profiles).reshape(nb, 8, cells_z)
-
-    found = jnp.sum(jnp.where(hits, 1.0, 0.0), axis=1, keepdims=True)
-    pressed = jnp.sum(jnp.where(hits, bp_ref[...], 0.0), axis=1, keepdims=True)
-    mask_ref[...] = jnp.broadcast_to(found, (columns, cells_z)).reshape(cells_x, cells_y, cells_z)
-    imposed_ref[...] = jnp.broadcast_to(1.0 + DENSITY_SCALE * pressed, (columns, cells_z)).reshape(
-        cells_x, cells_y, cells_z
-    )
-
+    loads = [
+        pltpu.make_async_copy(src, dst, load_s.at[n])
+        for n, (src, dst) in enumerate(
+            [
+                (pop_hbm, pop_ref),
+                (solid_hbm, solid_ref),
+                (bp_hbm, bp_ref),
+                (col_hbm, col_ref),
+                (dest_hbm, dest_ref),
+                (seg_hbm, seg_ref),
+                (segp_hbm, segp_ref),
+                (rate_hbm, stage.at[0]),
+                (leak_hbm, stage.at[1]),
+                (w_hbm, w_ref),
+                (mem_hbm, mem_ref),
+                (arity_hbm, arity_ref),
+                (res_hbm, res_ref),
+                (cross_hbm, cross_ref),
+            ]
+        )
+    ]
+    for n in (11, 12, 13, 4, 5, 3, 2, 0, 10, 6, 7, 8, 1, 9):
+        loads[n].start()
+
+    for n in (11, 12, 13):
+        loads[n].wait()
     live = [jnp.where(arity_ref[...] > k, 1.0, 0.0) for k in range(4)]
     pairs = off_diagonals(
         live,
@@ -265,26 +279,71 @@
         gbuf[0, n : n + 1, :] = value
     gbuf[0, 6:8, :] = jnp.zeros((2, junctions), F32)
 
-    ptab[y, hi] = segp_ref[...]
-    rate2[hi] = rate_ref[...]
-    leak2[hi] = leak_ref[...]
+    for n in (2, 3, 4, 5, 0):
+        loads[n].wait()
+    dest = dest_ref[...]
+    eye = iota((blocks, blocks), 0) == iota((blocks, blocks), 1)
+    dest_column = jnp.sum(jnp.where(eye, dest, 0), axis=1, keepdims=True)
+    earlier = jnp.logical_and(dest_column == dest, iota((blocks, blocks), 0) < iota((blocks, blocks), 1))
+    slot = jnp.sum(jnp.where(earlier, 1, 0), axis=0, keepdims=True)
+    slot_column = jnp.sum(jnp.where(eye, slot, 0), axis=1, keepdims=True)
+    number_column = jnp.sum(jnp.where(eye, seg_ref[...] + 1, 0), axis=1, keepdims=True)
+    r = iota((nb * 4, blocks), 0)
+    aimed = (r >> 2) == dest
+    chosen = jnp.where(jnp.logical_and(aimed, (r & 3) == slot), 1.0, 0.0)
+    pick[...] = chosen
+    columns = cells_x * cells_y
+    hits = iota((columns, blocks), 0) == col_ref[...]
+    selector = lax.dot_general(
+        chosen.astype(BF16),
+        jnp.where(hits, 1.0, 0.0).astype(BF16),
+        (((1,), (1,)), ((), ())),
+        preferred_element_type=F32,
+    ).astype(BF16)
+    axial = jnp.zeros((columns, cells_z), F32)
+    for i, c in enumerate(VELOCITIES):
+        if c[0]:
+            weight = c[0] * (1.0 / 18.0 if i < 7 else 1.0 / 36.0)
+            axial = axial + weight * pop_ref[i].reshape(columns, cells_z)
+    profiles = jnp.dot(
+        jnp.concatenate([selector] * 3, axis=1),
+        jnp.concatenate(split3(axial), axis=0),
+        preferred_element_type=F32,
+    )
+    number = jnp.where(iota((blocks, cells_z), 1) == slot_column, number_column, 0)
+    numbers = jnp.dot(
+        jnp.concatenate([jnp.where(aimed, 1.0, 0.0).astype(BF16)] * 2, axis=1),
+        jnp.concatenate([(number >> 6).astype(F32) * 64.0, (number & 63).astype(F32)], axis=0).astype(BF16),
+        preferred_element_type=F32,
+    )
+    is_label = (iota((nb * 4, cells_z), 0) & 3) == 3
+    msg[...] = jnp.where(is_label, numbers - 1.0, profiles).reshape(nb, 4, cells_z)
+
+    found = jnp.sum(jnp.where(hits, 1.0, 0.0), axis=1, keepdims=True)
+    pressed = jnp.sum(jnp.where(hits, bp_ref[...], 0.0), axis=1, keepdims=True)
+    mask_ref[...] = jnp.broadcast_to(found, (columns, cells_z)).reshape(cells_x, cells_y, cells_z)
+    imposed_ref[...] = jnp.broadcast_to(1.0 + DENSITY_SCALE * pressed, (columns, cells_z)).reshape(
+        cells_x, cells_y, cells_z
+    )
+
+    for n in (6, 7, 8, 10):
+        loads[n].wait()
+    ptab[s] = segp_ref[...]
+    rates[s] = stage[...]
 
     pl.semaphore_wait(barrier, nb - 1 + ns - 1 + len(CORNERS))
 
+    pair = [
+        copy(mem_ref, other_mem, pair_s.at[0], pair_r.at[0], partner),
+        copy(gbuf.at[0], gbuf.at[1], pair_s.at[1], pair_r.at[1], partner),
+    ]
+    for c in pair:
+        c.start()
     first = [
-        copy(segp_ref, ptab.at[y, hi], first_s.at[k - 1], first_r.at[k - 1], at(0, k)) for k in range(1, ns)
+        copy(segp_ref, ptab.at[s], first_s.at[k - 1], first_r.at[k - 1], at(0, k)) for k in range(1, ns)
     ]
     for c in first:
         c.start()
-    pair = [
-        copy(mem_ref, other_mem, pair_s.at[0], pair_r.at[0], partner),
-        copy(gbuf.at[0], gbuf.at[1], pair_s.at[1], pair_r.at[1], partner),
-        copy(rate_ref, rate2.at[hi], pair_s.at[2], pair_r.at[2], partner),
-        copy(leak_ref, leak2.at[hi], pair_s.at[3], pair_r.at[3], partner),
-    ]
-    for c in pair:
-        c.start()
-    pair_inflow = copy(flow, inflow2.at[hi], pair_s.at[4], pair_r.at[4], partner)
 
     def message(k):
         target = lax.rem(b + k, nb)
@@ -300,6 +359,11 @@
 
     lax.fori_loop(1, nb, start_message, 0)
     arrived[b] = msg[b]
+    second = [
+        copy(stage, rates.at[s], rates_s.at[k - 1], rates_r.at[k - 1], at(0, k)) for k in range(1, ns)
+    ]
+    for c in second:
+        c.start()
 
     def halo(parity):
         copies = [
@@ -318,6 +382,11 @@
             )
         return out
 
+    def start_halo(parity):
+        copies = halo(parity)
+        for n in (2, 3, 4, 5, 6, 7, 0, 1):
+            copies[n].start()
+
     halves = cells_y // 8
 
     def collide(source):
@@ -335,10 +404,6 @@
         lax.fori_loop(0, cells_x * halves, tile, 0)
 
     def pack():
-        for n, i in enumerate(X_UP):
-            sxu[n] = post[i, cells_x - 1]
-        for n, i in enumerate(X_DOWN):
-            sxd[n] = post[i, 0]
         for n, i in enumerate(Y_UP):
             for x in range(cells_x):
                 syu[n, x : x + 1, :] = post[i, x, cells_y - 1 : cells_y, :]
@@ -349,6 +414,10 @@
             x = cells_x - 1 if cx > 0 else 0
             row = cells_y - 1 if cy > 0 else 0
             sc[n] = jnp.broadcast_to(post[i, x, row : row + 1, :], (8, cells_z))
+        for n, i in enumerate(X_UP):
+            sxu[n] = post[i, cells_x - 1]
+        for n, i in enumerate(X_DOWN):
+            sxd[n] = post[i, 0]
 
     def stream(parity):
         edge = iota((cells_y, cells_z), 0)
@@ -376,22 +445,25 @@
                     value = pltpu.roll(value, cz % cells_z, 1)
                 pop_out[i, x] = value
 
+    loads[1].wait()
     collide(pop_ref)
     pack()
-    for c in halo(0):
-        c.start()
+    start_halo(0)
 
     def build(n, ref):
         m = jnp.concatenate([ref[k : k + 1, :] for k in range(4)], axis=1)
-        per = rows * 128
-        sub = m // per
-        row = (lax.rem(sub, ny) * 2 + sub // ny) * rows + (lax.rem(m, per) >> 7)
+        row = m >> 7
         row_at[n] = row
         lines = iota((128, links), 0)
         oh_c[n] = jnp.where(lines == (m & 127), 1.0, 0.0).astype(BF16)
         oh_r[n] = jnp.where(iota((ns * rows, links), 0) == row, 1.0, 0.0).astype(BF16)
 
     build(0, mem_ref)
+    loads[9].wait()
+    high, low = split2(w_ref[...])
+    w_parts[:, 0:cells_z] = high
+    w_parts[:, cells_z : 2 * cells_z] = low
+    w_parts[:, 2 * cells_z : 3 * cells_z] = high
     pair[0].wait()
     build(1, other_mem)
     for c in pair[1:]:
@@ -426,38 +498,50 @@
             return carry
 
         lax.fori_loop(1, nb, wait_message, 0)
-        got = arrived[...].reshape(nb * 8, cells_z)
-        numbers = pltpu.roll(got, nb * 8 - 4, 0)
-        at_row = iota((nb * 8, cells_z), 0)
-        holds = jnp.logical_and((at_row & 4) == 0, (at_row & 3) < SLOTS)
-        numbers = jnp.where(holds, numbers.astype(jnp.int32), -1)
+        got = arrived[...].reshape(nb * 4, cells_z)
+        at_row = iota((nb * 4, cells_z), 0) & 3
+        labels = jnp.where(
+            at_row == 0,
+            pltpu.roll(got, nb * 4 - 3, 0),
+            jnp.where(at_row == 1, pltpu.roll(got, nb * 4 - 2, 0), pltpu.roll(got, nb * 4 - 1, 0)),
+        )
+        labels = jnp.where(iota((nb * 4, cells_z), 1) == at_row, labels, 0.0)
+        numbers = jnp.sum(labels, axis=1, keepdims=True).astype(jnp.int32)
+        numbers = jnp.where(at_row < SLOTS, jnp.broadcast_to(numbers, (nb * 4, 128)), -1)
         ids_ref[...] = numbers
-        lane = iota((nb * 8, 128), 1)
-
-        def chunk(n, carry):
-            weights = w_ref[pl.ds(pl.multiple_of(n * 128, 128), 128), :]
-            value = lax.dot_general(
-                got, weights, (((1,), (1,)), ((), ())), precision=HIGHEST, preferred_element_type=F32
-            )
-            value = jnp.where(numbers == lane + n * 128, value, 0.0)
-            flow[pl.ds(n, 1), :] = jnp.sum(value, axis=0, keepdims=True)
-            return carry
-
-        lax.fori_loop(0, rows, chunk, 0)
-        pair_inflow.start()
-        inflow2[hi] = flow[...]
-        pair_inflow.wait()
+        lane = iota((nb * 4, 128), 1)
+        high, low = split2(got)
+        value = lax.dot_general(
+            jnp.concatenate([high, high, low], axis=1),
+            w_parts[...],
+            (((1,), (1,)), ((), ())),
+            preferred_element_type=F32,
+        )
+        for n in range(rows):
+            mine = jnp.where(numbers == lane + n * 128, value[:, n * 128 : (n + 1) * 128], 0.0)
+            flow[n : n + 1, :] = jnp.sum(mine, axis=0, keepdims=True)
+        third = [
+            copy(flow, inflow_all.at[s], inflow_s.at[k - 1], inflow_r.at[k - 1], at(0, k))
+            for k in range(1, ns)
+        ]
+        for c in third:
+            c.start()
+        inflow_all[s] = flow[...]
+        for c in second:
+            c.wait()
+        for c in third:
+            c.wait()
 
     def step(t, carry):
         parity = lax.rem(t, 2)
         table = jnp.concatenate(split2(ptab[...].reshape(ns * rows, 128)), axis=1)
         both = flows(0, table) + flows(1, table)
-        part[...] = (both[:, :128] + both[:, 128:]).reshape(ny, 2, rows, 128)
-        scatter = [
-            copy(part.at[lax.rem(y + k, ny)], rs.at[k - 1], rs_s.at[k - 1], rs_r.at[k - 1], ring(k))
+        part[parity, y] = both[:, :128] + both[:, 128:]
+        partial = [
+            copy(part.at[parity, y], part.at[parity, y], part_s.at[k - 1], part_r.at[parity, k - 1], ring(k))
             for k in range(1, ny)
         ]
-        for c in scatter:
+        for c in partial:
             c.start()
 
         now = halo(parity)
@@ -471,44 +555,35 @@
         def _():
             collide(pop_out)
             pack()
-            for c in halo(1 - parity):
-                c.start()
+            start_halo(1 - parity)
 
         @pl.when(t == 0)
         def _():
             inflows()
 
-        for c in scatter:
+        for c in partial:
             c.wait()
-        balance = part[y]
+        balance = part[parity, 0]
         for k in range(1, ny):
-            balance = balance + rs[k - 1]
-        p = ptab[y]
-        ptab[y] = p + rate2[...] * (inflow2[...] - balance - leak2[...] * p)
-
-        @pl.when(t < STEPS - 1)
-        def _():
-            gather = [
-                copy(ptab.at[y], ptab.at[y], ag_s.at[k - 1], ag_r.at[k - 1], ring(k)) for k in range(1, ny)
-            ]
-            for c in gather:
-                c.start()
-            for c in gather:
-                c.wait()
-
+            balance = balance + part[parity, k]
+        p = ptab[...].reshape(ns * rows, 128)
+        rate = rates[:, 0].reshape(ns * rows, 128)
+        leak = rates[:, 1].reshape(ns * rows, 128)
+        source = inflow_all[...].reshape(ns * rows, 128)
+        ptab[...] = (p + rate * (source - balance - leak * p)).reshape(ns, rows, 128)
         return carry
 
     lax.fori_loop(0, STEPS, step, 0)
-    final = ptab[y, hi]
+    final = ptab[s]
     seg_out[...] = final
 
     numbers = ids_ref[...]
-    lane = iota((nb * 8, 128), 1)
-    value = jnp.zeros((nb * 8, 128), F32)
+    lane = iota((nb * 4, 128), 1)
+    value = jnp.zeros((nb * 4, 128), F32)
     for n in range(rows):
         value = value + jnp.where(numbers == lane + n * 128, final[n : n + 1, :], 0.0)
     value = jnp.sum(value, axis=1, keepdims=True)
-    ret_out[...] = jnp.broadcast_to(value, (nb * 8, 128)).reshape(nb, 8, 128)
+    ret_out[...] = jnp.broadcast_to(value, (nb * 4, 128)).reshape(nb, 4, 128)
 
     def start_answer(k, carry):
         answer(k).start()
@@ -521,11 +596,22 @@
     lax.fori_loop(1, nb, start_answer, 0)
     ret_in[b] = ret_out[b]
     lax.fori_loop(1, nb, wait_answer, 0)
-    back = ret_in[...].reshape(nb * 8, 128)[:, :blocks]
-    is_value = (iota((nb * 8, blocks), 0) & 4) == 0
-    bp_out[...] = jnp.sum(
-        jnp.where(jnp.logical_and(is_value, pick[...] > 0.5), back, 0.0), axis=0, keepdims=True
-    )
+    back = ret_in[...].reshape(nb * 4, 128)[:, :blocks]
+    bp_out[...] = jnp.sum(jnp.where(pick[...] > 0.5, back, 0.0), axis=0, keepdims=True)
+
+
+def finish(pop_in, seg_in, bp_in, pop_out, seg_out, bp_out, pop_hold, seg_hold, bp_hold, load_s, store_s):
+    parts = [(pop_in.at[i], pop_hold.at[i], pop_out.at[i]) for i in range(pop_in.shape[0])]
+    parts += [(seg_in, seg_hold, seg_out), (bp_in, bp_hold, bp_out)]
+    loads = [pltpu.make_async_copy(a, b, load_s.at[n]) for n, (a, b, _) in enumerate(parts)]
+    stores = [pltpu.make_async_copy(b, c, store_s.at[n]) for n, (_, b, c) in enumerate(parts)]
+    for c in loads:
+        c.start()
+    for load, store in zip(loads, stores):
+        load.wait()
+        store.start()
+    for c in stores:
+        c.wait()
 
 
 def local(
@@ -552,6 +638,19 @@
     vmem, dma = pltpu.VMEM, pltpu.SemaphoreType.DMA
     scratch = [
         vmem((19, cx, cy, cz), F32),
+        vmem((cx, cy, cz), jnp.int32),
+        vmem((1, blocks), F32),
+        vmem((1, blocks), jnp.int32),
+        vmem((1, blocks), jnp.int32),
+        vmem((1, blocks), jnp.int32),
+        vmem((rows, 128), F32),
+        vmem((segs, cz), F32),
+        vmem((4, junctions), jnp.int32),
+        vmem((1, junctions), jnp.int32),
+        vmem((4, junctions), F32),
+        vmem((4, 4, junctions), F32),
+        dma((14,)),
+        vmem((19, cx, cy, cz), F32),
         vmem((cx, cy, cz), F32),
         vmem((cx, cy, cz), F32),
         vmem((5, cy, cz), F32),
@@ -564,34 +663,36 @@
         vmem((2, 5, cx, cz), F32),
         vmem((2, 5, cx, cz), F32),
         vmem((2, 4, 8, cz), F32),
-        vmem((ny, 2, rows, 128), F32),
+        vmem((ns, rows, 128), F32),
         vmem((2, rows, 128), F32),
-        vmem((2, rows, 128), F32),
-        vmem((2, rows, 128), F32),
+        vmem((ns, 2, rows, 128), F32),
+        vmem((ns, rows, 128), F32),
         vmem((rows, 128), F32),
         vmem((4, junctions), jnp.int32),
         vmem((2, 8, junctions), F32),
         vmem((2, 1, links), jnp.int32),
         vmem((2, 128, links), BF16),
         vmem((2, ns * rows, links), BF16),
-        vmem((ny, 2, rows, 128), F32),
-        vmem((ny - 1, 2, rows, 128), F32),
-        vmem((nb, 8, cz), F32),
-        vmem((nb, 8, cz), F32),
-        vmem((nb * 8, blocks), F32),
-        vmem((nb * 8, cz), jnp.int32),
-        vmem((nb, 8, 128), F32),
-        vmem((nb, 8, 128), F32),
+        vmem((2, ny, ns * rows, 128), F32),
+        vmem((nb, 4, cz), F32),
+        vmem((nb, 4, cz), F32),
+        vmem((nb * 4, blocks), F32),
+        vmem((nb * 4, cz), jnp.int32),
+        vmem((segs, 3 * cz), BF16),
+        vmem((nb, 4, 128), F32),
+        vmem((nb, 4, 128), F32),
         dma((8,)),
         dma((2, 8)),
         dma((ns - 1,)),
         dma((ns - 1,)),
-        dma((5,)),
-        dma((5,)),
+        dma((ns - 1,)),
+        dma((ns - 1,)),
+        dma((ns - 1,)),
+        dma((ns - 1,)),
+        dma((2,)),
+        dma((2,)),
         dma((ny - 1,)),
-        dma((ny - 1,)),
-        dma((ny - 1,)),
-        dma((ny - 1,)),
+        dma((2, ny - 1)),
         dma((nb - 1,)),
         dma((nb - 1,)),
         dma((nb - 1,)),
@@ -605,11 +706,11 @@
             jax.ShapeDtypeStruct((rows, 128), F32),
             jax.ShapeDtypeStruct((1, blocks), F32),
         ),
-        in_specs=[spec] * 14,
+        in_specs=[pl.BlockSpec(memory_space=pltpu.HBM)] * 14,
         out_specs=(spec, spec, spec),
         scratch_shapes=scratch,
         compiler_params=pltpu.CompilerParams(
-            collective_id=0, has_side_effects=True, vmem_limit_bytes=48 * 2**20
+            collective_id=0, has_side_effects=True, vmem_limit_bytes=56 * 2**20
         ),
         name="coupled",
     )(
@@ -628,6 +729,26 @@
         junc_res,
         junc_cross,
     )
+    hbm = pl.BlockSpec(memory_space=pltpu.HBM)
+    lattice, pressure, back = pl.pallas_call(
+        finish,
+        out_shape=(
+            jax.ShapeDtypeStruct(populations.shape, F32),
+            jax.ShapeDtypeStruct((rows, 128), F32),
+            jax.ShapeDtypeStruct((1, blocks), F32),
+        ),
+        in_specs=[hbm] * 3,
+        out_specs=(hbm, hbm, hbm),
+        scratch_shapes=[
+            vmem(populations.shape, F32),
+            vmem((rows, 128), F32),
+            vmem((1, blocks), F32),
+            dma((21,)),
+            dma((21,)),
+        ],
+        compiler_params=pltpu.CompilerParams(vmem_limit_bytes=56 * 2**20),
+        name="finish",
+    )(lattice, pressure, back)
     return lattice, pressure.reshape(segs), back.reshape(blocks)
 
 

time: 101 us -> 80.2 us (0.79)
  Pallas kernels: 90.4 us -> 79.4 us
  local copies, waits for them, and re-layouts: 9.35 us -> 0 us
    pallas_call x1, Pallas kernels: 90.4 us -> 77.4 us  [local(): pl.pallas_call(functools.partial(kernel, nb, ns), out_shape=(jax.ShapeDty...]
    unnamed x31 -> x0, local copies, waits for them, and re-layouts: 9.35 us -> none
    pallas_call x0 -> x1, Pallas kernels: none -> 2.03 us  [local(): pl.pallas_call(finish, out_shape=(jax.ShapeDtypeStruct(populations.shape,...]
where the time goes in v2:
time: 80.2 us; the launch traced here: 80 us
  Pallas kernels  79.4 us (99%)
    pallas_call x1, Pallas kernels, local(): pl.pallas_call(functools.partial(kernel, nb, ns), out_shape=(jax.ShapeDty...  77.4 us
    pallas_call x1, Pallas kernels, local(): pl.pallas_call(finish, out_shape=(jax.ShapeDtypeStruct(populations.shape,...  2.03 us

profile of v2, /device:TPU:1, one launch (start us, length us, event | category | flops | bytes accessed | tf_op | source)
XLA Modules:
  0.0 80.0 jit_solution(1355133140532205782)
XLA Ops:
  0.6 77.4 %coupled.1 = (f32[19,4,16,128]{3,2,1,0:T(8,128)}, f32[16,128]{1,0:T(8,128)}, f32[1,32]{1,0:T(1,128)}) custom-call(f32[19,4,16,128]{3,2,1,0:T(8,128)} %pop_hbm.1, s32[4,16,128]{2,1,0:T(8,128)} %solid_hbm.1, f32[1,32]{1,0:T(1,128)} %bitcast.14, s32[1,32]{1,0:T(1,128)} %bitcast.15, s32[1,32]{1,0:T(1,128)} %bitcast.16, s32[1,32]{1,0:T(1,128)} %bitcast.17, ...), custom_call_target="tpu_custom_call" | custom-call | tf_op jit(solution)/shard_map/coupled/pallas_call | solution.py:702
  78.0 2.0 %finish.1 = (f32[19,4,16,128]{3,2,1,0:T(8,128)}, f32[16,128]{1,0:T(8,128)}, f32[1,32]{1,0:T(1,128)}) custom-call(f32[19,4,16,128]{3,2,1,0:T(8,128)} %get-tuple-element.9.pop_in, f32[16,128]{1,0:T(8,128)} %get-tuple-element.10.seg_in, f32[1,32]{1,0:T(1,128)} %get-tuple-element.11.bp_in), custom_call_target="tpu_custom_call" | custom-call | tf_op jit(solution)/shard_map/finish/pallas_call | solution.py:733

commit v3 on v2

--- a/solution.py
+++ b/solution.py
@@ -267,104 +267,6 @@
     for n in (11, 12, 13, 4, 5, 3, 2, 0, 10, 6, 7, 8, 1, 9):
         loads[n].start()
 
-    for n in (11, 12, 13):
-        loads[n].wait()
-    live = [jnp.where(arity_ref[...] > k, 1.0, 0.0) for k in range(4)]
-    pairs = off_diagonals(
-        live,
-        [res_ref[k : k + 1, :] for k in range(4)],
-        [[cross_ref[k, l : l + 1, :] for l in range(4)] for k in range(4)],
-    )
-    for n, value in enumerate(pairs):
-        gbuf[0, n : n + 1, :] = value
-    gbuf[0, 6:8, :] = jnp.zeros((2, junctions), F32)
-
-    for n in (2, 3, 4, 5, 0):
-        loads[n].wait()
-    dest = dest_ref[...]
-    eye = iota((blocks, blocks), 0) == iota((blocks, blocks), 1)
-    dest_column = jnp.sum(jnp.where(eye, dest, 0), axis=1, keepdims=True)
-    earlier = jnp.logical_and(dest_column == dest, iota((blocks, blocks), 0) < iota((blocks, blocks), 1))
-    slot = jnp.sum(jnp.where(earlier, 1, 0), axis=0, keepdims=True)
-    slot_column = jnp.sum(jnp.where(eye, slot, 0), axis=1, keepdims=True)
-    number_column = jnp.sum(jnp.where(eye, seg_ref[...] + 1, 0), axis=1, keepdims=True)
-    r = iota((nb * 4, blocks), 0)
-    aimed = (r >> 2) == dest
-    chosen = jnp.where(jnp.logical_and(aimed, (r & 3) == slot), 1.0, 0.0)
-    pick[...] = chosen
-    columns = cells_x * cells_y
-    hits = iota((columns, blocks), 0) == col_ref[...]
-    selector = lax.dot_general(
-        chosen.astype(BF16),
-        jnp.where(hits, 1.0, 0.0).astype(BF16),
-        (((1,), (1,)), ((), ())),
-        preferred_element_type=F32,
-    ).astype(BF16)
-    axial = jnp.zeros((columns, cells_z), F32)
-    for i, c in enumerate(VELOCITIES):
-        if c[0]:
-            weight = c[0] * (1.0 / 18.0 if i < 7 else 1.0 / 36.0)
-            axial = axial + weight * pop_ref[i].reshape(columns, cells_z)
-    profiles = jnp.dot(
-        jnp.concatenate([selector] * 3, axis=1),
-        jnp.concatenate(split3(axial), axis=0),
-        preferred_element_type=F32,
-    )
-    number = jnp.where(iota((blocks, cells_z), 1) == slot_column, number_column, 0)
-    numbers = jnp.dot(
-        jnp.concatenate([jnp.where(aimed, 1.0, 0.0).astype(BF16)] * 2, axis=1),
-        jnp.concatenate([(number >> 6).astype(F32) * 64.0, (number & 63).astype(F32)], axis=0).astype(BF16),
-        preferred_element_type=F32,
-    )
-    is_label = (iota((nb * 4, cells_z), 0) & 3) == 3
-    msg[...] = jnp.where(is_label, numbers - 1.0, profiles).reshape(nb, 4, cells_z)
-
-    found = jnp.sum(jnp.where(hits, 1.0, 0.0), axis=1, keepdims=True)
-    pressed = jnp.sum(jnp.where(hits, bp_ref[...], 0.0), axis=1, keepdims=True)
-    mask_ref[...] = jnp.broadcast_to(found, (columns, cells_z)).reshape(cells_x, cells_y, cells_z)
-    imposed_ref[...] = jnp.broadcast_to(1.0 + DENSITY_SCALE * pressed, (columns, cells_z)).reshape(
-        cells_x, cells_y, cells_z
-    )
-
-    for n in (6, 7, 8, 10):
-        loads[n].wait()
-    ptab[s] = segp_ref[...]
-    rates[s] = stage[...]
-
-    pl.semaphore_wait(barrier, nb - 1 + ns - 1 + len(CORNERS))
-
-    pair = [
-        copy(mem_ref, other_mem, pair_s.at[0], pair_r.at[0], partner),
-        copy(gbuf.at[0], gbuf.at[1], pair_s.at[1], pair_r.at[1], partner),
-    ]
-    for c in pair:
-        c.start()
-    first = [
-        copy(segp_ref, ptab.at[s], first_s.at[k - 1], first_r.at[k - 1], at(0, k)) for k in range(1, ns)
-    ]
-    for c in first:
-        c.start()
-
-    def message(k):
-        target = lax.rem(b + k, nb)
-        return copy(msg.at[target], arrived.at[b], msg_s.at[k - 1], msg_r.at[k - 1], (target, s))
-
-    def answer(k):
-        target = lax.rem(b + k, nb)
-        return copy(ret_out.at[target], ret_in.at[b], ret_s.at[k - 1], ret_r.at[k - 1], (target, s))
-
-    def start_message(k, carry):
-        message(k).start()
-        return carry
-
-    lax.fori_loop(1, nb, start_message, 0)
-    arrived[b] = msg[b]
-    second = [
-        copy(stage, rates.at[s], rates_s.at[k - 1], rates_r.at[k - 1], at(0, k)) for k in range(1, ns)
-    ]
-    for c in second:
-        c.start()
-
     def halo(parity):
         copies = [
             (sxu, rxu, (1, 0)),
@@ -445,11 +347,6 @@
                     value = pltpu.roll(value, cz % cells_z, 1)
                 pop_out[i, x] = value
 
-    loads[1].wait()
-    collide(pop_ref)
-    pack()
-    start_halo(0)
-
     def build(n, ref):
         m = jnp.concatenate([ref[k : k + 1, :] for k in range(4)], axis=1)
         row = m >> 7
@@ -458,18 +355,149 @@
         oh_c[n] = jnp.where(lines == (m & 127), 1.0, 0.0).astype(BF16)
         oh_r[n] = jnp.where(iota((ns * rows, links), 0) == row, 1.0, 0.0).astype(BF16)
 
-    build(0, mem_ref)
-    loads[9].wait()
-    high, low = split2(w_ref[...])
-    w_parts[:, 0:cells_z] = high
-    w_parts[:, cells_z : 2 * cells_z] = low
-    w_parts[:, 2 * cells_z : 3 * cells_z] = high
-    pair[0].wait()
-    build(1, other_mem)
-    for c in pair[1:]:
-        c.wait()
+    columns = cells_x * cells_y
+
+    def hit():
+        return iota((columns, blocks), 0) == col_ref[...]
+
+    def prepare_junctions():
+        for n in (11, 12, 13):
+            loads[n].wait()
+        live = [jnp.where(arity_ref[...] > k, 1.0, 0.0) for k in range(4)]
+        pairs = off_diagonals(
+            live,
+            [res_ref[k : k + 1, :] for k in range(4)],
+            [[cross_ref[k, l : l + 1, :] for l in range(4)] for k in range(4)],
+        )
+        for n, value in enumerate(pairs):
+            gbuf[0, n : n + 1, :] = value
+        gbuf[0, 6:8, :] = jnp.zeros((2, junctions), F32)
+
+    def prepare_lattice():
+        for n in (0, 1, 2, 3):
+            loads[n].wait()
+        hits = hit()
+        found = jnp.sum(jnp.where(hits, 1.0, 0.0), axis=1, keepdims=True)
+        pressed = jnp.sum(jnp.where(hits, bp_ref[...], 0.0), axis=1, keepdims=True)
+        mask_ref[...] = jnp.broadcast_to(found, (columns, cells_z)).reshape(cells_x, cells_y, cells_z)
+        imposed_ref[...] = jnp.broadcast_to(1.0 + DENSITY_SCALE * pressed, (columns, cells_z)).reshape(
+            cells_x, cells_y, cells_z
+        )
+        collide(pop_ref)
+        pack()
+
+    def prepare_messages():
+        for n in (4, 5):
+            loads[n].wait()
+        dest = dest_ref[...]
+        eye = iota((blocks, blocks), 0) == iota((blocks, blocks), 1)
+        dest_column = jnp.sum(jnp.where(eye, dest, 0), axis=1, keepdims=True)
+        earlier = jnp.logical_and(dest_column == dest, iota((blocks, blocks), 0) < iota((blocks, blocks), 1))
+        slot = jnp.sum(jnp.where(earlier, 1, 0), axis=0, keepdims=True)
+        slot_column = jnp.sum(jnp.where(eye, slot, 0), axis=1, keepdims=True)
+        number_column = jnp.sum(jnp.where(eye, seg_ref[...] + 1, 0), axis=1, keepdims=True)
+        r = iota((nb * 4, blocks), 0)
+        aimed = (r >> 2) == dest
+        chosen = jnp.where(jnp.logical_and(aimed, (r & 3) == slot), 1.0, 0.0)
+        pick[...] = chosen
+        hits = hit()
+        selector = lax.dot_general(
+            chosen.astype(BF16),
+            jnp.where(hits, 1.0, 0.0).astype(BF16),
+            (((1,), (1,)), ((), ())),
+            preferred_element_type=F32,
+        ).astype(BF16)
+        axial = jnp.zeros((columns, cells_z), F32)
+        for i, c in enumerate(VELOCITIES):
+            if c[0]:
+                weight = c[0] * (1.0 / 18.0 if i < 7 else 1.0 / 36.0)
+                axial = axial + weight * pop_ref[i].reshape(columns, cells_z)
+        profiles = jnp.dot(
+            jnp.concatenate([selector] * 3, axis=1),
+            jnp.concatenate(split3(axial), axis=0),
+            preferred_element_type=F32,
+        )
+        number = jnp.where(iota((blocks, cells_z), 1) == slot_column, number_column, 0)
+        numbers = jnp.dot(
+            jnp.concatenate([jnp.where(aimed, 1.0, 0.0).astype(BF16)] * 2, axis=1),
+            jnp.concatenate([(number >> 6).astype(F32) * 64.0, (number & 63).astype(F32)], axis=0).astype(BF16),
+            preferred_element_type=F32,
+        )
+        is_label = (iota((nb * 4, cells_z), 0) & 3) == 3
+        msg[...] = jnp.where(is_label, numbers - 1.0, profiles).reshape(nb, 4, cells_z)
+
+    def prepare_network():
+        for n in (6, 7, 8, 10):
+            loads[n].wait()
+        ptab[s] = segp_ref[...]
+        rates[s] = stage[...]
+        build(0, mem_ref)
+        loads[9].wait()
+        high, low = split2(w_ref[...])
+        w_parts[:, 0:cells_z] = high
+        w_parts[:, cells_z : 2 * cells_z] = low
+        w_parts[:, 2 * cells_z : 3 * cells_z] = high
+
+    pair = [
+        copy(mem_hbm, other_mem, pair_s.at[0], pair_r.at[0], partner),
+        copy(gbuf.at[0], gbuf.at[1], pair_s.at[1], pair_r.at[1], partner),
+    ]
+    first = [
+        copy(segp_hbm, ptab.at[s], first_s.at[k - 1], first_r.at[k - 1], at(0, k)) for k in range(1, ns)
+    ]
+    second = [
+        copy(stage, rates.at[s], rates_s.at[k - 1], rates_r.at[k - 1], at(0, k)) for k in range(1, ns)
+    ]
+
+    def message(k):
+        target = lax.rem(b + k, nb)
+        return copy(msg.at[target], arrived.at[b], msg_s, msg_r, (target, s))
+
+    def answer(k):
+        target = lax.rem(b + k, nb)
+        return copy(ret_out.at[target], ret_in.at[b], ret_s, ret_r, (target, s))
+
+    def start_message(k, carry):
+        message(lax.rem(k + nb // 4, nb - 1) + 1).start()
+        return carry
+
+    early, late = hi == 0, hi != 0
+
+    @pl.when(early)
+    def _():
+        prepare_junctions()
+        prepare_lattice()
+        prepare_messages()
+        prepare_network()
+
+    pl.semaphore_wait(barrier, nb - 1 + ns - 1 + len(CORNERS))
+
+    pair[0].start()
     for c in first:
-        c.wait()
+        c.start()
+
+    @pl.when(late)
+    def _():
+        prepare_junctions()
+
+    pair[1].start()
+
+    @pl.when(late)
+    def _():
+        prepare_lattice()
+
+    start_halo(0)
+
+    @pl.when(late)
+    def _():
+        prepare_messages()
+
+    lax.fori_loop(1, nb, start_message, 0)
+    arrived[b] = msg[b]
+
+    @pl.when(late)
+    def _():
+        prepare_network()
 
     def flows(n, table):
         members = oh_c[n]
@@ -493,11 +521,8 @@
         )
 
     def inflows():
-        def wait_message(k, carry):
-            message(k).wait()
-            return carry
-
-        lax.fori_loop(1, nb, wait_message, 0)
+        whole = pl.ds(0, nb - 1)
+        copy(msg.at[whole], arrived.at[whole], msg_s, msg_r, at(1, 0)).wait()
         got = arrived[...].reshape(nb * 4, cells_z)
         at_row = iota((nb * 4, cells_z), 0) & 3
         labels = jnp.where(
@@ -532,11 +557,26 @@
         for c in third:
             c.wait()
 
+    def table_of():
+        return jnp.concatenate(split2(ptab[...].reshape(ns * rows, 128)), axis=1)
+
+    def joined(both):
+        return both[:, :128] + both[:, 128:]
+
+    for c in first:
+        c.wait()
+    table = table_of()
+    both = flows(0, table)
+    pair[0].wait()
+    build(1, other_mem)
+    pair[1].wait()
+    for c in second:
+        c.start()
+    both = both + flows(1, table)
+    part[0, y] = joined(both)
+
     def step(t, carry):
         parity = lax.rem(t, 2)
-        table = jnp.concatenate(split2(ptab[...].reshape(ns * rows, 128)), axis=1)
-        both = flows(0, table) + flows(1, table)
-        part[parity, y] = both[:, :128] + both[:, 128:]
         partial = [
             copy(part.at[parity, y], part.at[parity, y], part_s.at[k - 1], part_r.at[parity, k - 1], ring(k))
             for k in range(1, ny)
@@ -571,6 +611,12 @@
         leak = rates[:, 1].reshape(ns * rows, 128)
         source = inflow_all[...].reshape(ns * rows, 128)
         ptab[...] = (p + rate * (source - balance - leak * p)).reshape(ns, rows, 128)
+
+        @pl.when(t < STEPS - 1)
+        def _():
+            table = table_of()
+            part[1 - parity, y] = joined(flows(0, table) + flows(1, table))
+
         return carry
 
     lax.fori_loop(0, STEPS, step, 0)
@@ -586,31 +632,24 @@
     ret_out[...] = jnp.broadcast_to(value, (nb * 4, 128)).reshape(nb, 4, 128)
 
     def start_answer(k, carry):
-        answer(k).start()
-        return carry
-
-    def wait_answer(k, carry):
-        answer(k).wait()
+        answer(lax.rem(k + nb // 4, nb - 1) + 1).start()
         return carry
 
     lax.fori_loop(1, nb, start_answer, 0)
     ret_in[b] = ret_out[b]
-    lax.fori_loop(1, nb, wait_answer, 0)
+    whole = pl.ds(0, nb - 1)
+    copy(ret_out.at[whole], ret_in.at[whole], ret_s, ret_r, at(1, 0)).wait()
     back = ret_in[...].reshape(nb * 4, 128)[:, :blocks]
     bp_out[...] = jnp.sum(jnp.where(pick[...] > 0.5, back, 0.0), axis=0, keepdims=True)
 
 
-def finish(pop_in, seg_in, bp_in, pop_out, seg_out, bp_out, pop_hold, seg_hold, bp_hold, load_s, store_s):
-    parts = [(pop_in.at[i], pop_hold.at[i], pop_out.at[i]) for i in range(pop_in.shape[0])]
-    parts += [(seg_in, seg_hold, seg_out), (bp_in, bp_hold, bp_out)]
-    loads = [pltpu.make_async_copy(a, b, load_s.at[n]) for n, (a, b, _) in enumerate(parts)]
-    stores = [pltpu.make_async_copy(b, c, store_s.at[n]) for n, (_, b, c) in enumerate(parts)]
-    for c in loads:
+def finish(pop_in, seg_in, bp_in, pop_out, seg_out, bp_out, sems):
+    copies = [pltpu.make_async_copy(pop_in.at[i], pop_out.at[i], sems.at[i]) for i in range(pop_in.shape[0])]
+    copies.append(pltpu.make_async_copy(seg_in, seg_out, sems.at[len(copies)]))
+    copies.append(pltpu.make_async_copy(bp_in, bp_out, sems.at[len(copies)]))
+    for c in copies:
         c.start()
-    for load, store in zip(loads, stores):
-        load.wait()
-        store.start()
-    for c in stores:
+    for c in copies:
         c.wait()
 
 
@@ -693,18 +732,18 @@
         dma((2,)),
         dma((ny - 1,)),
         dma((2, ny - 1)),
-        dma((nb - 1,)),
-        dma((nb - 1,)),
-        dma((nb - 1,)),
-        dma((nb - 1,)),
+        dma,
+        dma,
+        dma,
+        dma,
     ]
     spec = pl.BlockSpec(memory_space=vmem)
     lattice, pressure, back = pl.pallas_call(
         functools.partial(kernel, nb, ns),
         out_shape=(
-            jax.ShapeDtypeStruct(populations.shape, F32),
-            jax.ShapeDtypeStruct((rows, 128), F32),
-            jax.ShapeDtypeStruct((1, blocks), F32),
+            pltpu.VMEM(populations.shape, F32),
+            pltpu.VMEM((rows, 128), F32),
+            pltpu.VMEM((1, blocks), F32),
         ),
         in_specs=[pl.BlockSpec(memory_space=pltpu.HBM)] * 14,
         out_specs=(spec, spec, spec),
@@ -737,16 +776,12 @@
             jax.ShapeDtypeStruct((rows, 128), F32),
             jax.ShapeDtypeStruct((1, blocks), F32),
         ),
-        in_specs=[hbm] * 3,
+        in_specs=[spec] * 3,
         out_specs=(hbm, hbm, hbm),
         scratch_shapes=[
-            vmem(populations.shape, F32),
-            vmem((rows, 128), F32),
-            vmem((1, blocks), F32),
-            dma((21,)),
             dma((21,)),
         ],
-        compiler_params=pltpu.CompilerParams(vmem_limit_bytes=56 * 2**20),
+        compiler_params=pltpu.CompilerParams(vmem_limit_bytes=2**20),
         name="finish",
     )(lattice, pressure, back)
     return lattice, pressure.reshape(segs), back.reshape(blocks)

time: 80.2 us -> 76.2 us (0.950)
  Pallas kernels: 79.4 us -> 75.4 us
    pallas_call x1, Pallas kernels: 77.4 us -> 74.4 us  [local(): pl.pallas_call(functools.partial(kernel, nb, ns), out_shape=(pltpu.VMEM(p...]
    pallas_call x1, Pallas kernels: 2.03 us -> 1 us  [local(): pl.pallas_call(finish, out_shape=(jax.ShapeDtypeStruct(populations.shape,...]
where the time goes in v3:
time: 76.2 us; the launch traced here: 76.1 us
  Pallas kernels  75.4 us (99%)
    pallas_call x1, Pallas kernels, local(): pl.pallas_call(functools.partial(kernel, nb, ns), out_shape=(pltpu.VMEM(p...  74.4 us

profile of v3, /device:TPU:1, one launch (start us, length us, event | category | flops | bytes accessed | tf_op | source)
XLA Modules:
  0.0 76.1 jit_solution(10913091470643891324)
XLA Ops:
  0.6 74.4 %coupled.1 = (f32[19,4,16,128]{3,2,1,0:T(8,128)S(1)}, f32[16,128]{1,0:T(8,128)S(1)}, f32[1,32]{1,0:T(1,128)S(1)}) custom-call(f32[19,4,16,128]{3,2,1,0:T(8,128)} %pop_hbm.1, s32[4,16,128]{2,1,0:T(8,128)} %solid_hbm.1, f32[1,32]{1,0:T(1,128)} %bitcast.14, s32[1,32]{1,0:T(1,128)} %bitcast.15, s32[1,32]{1,0:T(1,128)} %bitcast.16, s32[1,32]{1,0:T(1,128)} %bitcast.17, ...), custom_call_target="tpu_custom_call" | custom-call | tf_op jit(solution)/shard_map/coupled/pallas_call | solution.py:741
  75.1 1.0 %finish.1 = (f32[19,4,16,128]{3,2,1,0:T(8,128)}, f32[16,128]{1,0:T(8,128)}, f32[1,32]{1,0:T(1,128)}) custom-call(f32[19,4,16,128]{3,2,1,0:T(8,128)S(1)} %get-tuple-element.9.pop_in, f32[16,128]{1,0:T(8,128)S(1)} %get-tuple-element.10.seg_in, f32[1,32]{1,0:T(1,128)S(1)} %get-tuple-element.11.bp_in), custom_call_target="tpu_custom_call" | custom-call | tf_op jit(solution)/shard_map/finish/pallas_call | solution.py:772

commit v4 on v3

--- a/solution.py
+++ b/solution.py
@@ -188,7 +188,8 @@
     msg,
     arrived,
     pick,
-    ids_ref,
+    labels,
+    last,
     w_parts,
     ret_out,
     ret_in,
@@ -217,14 +218,14 @@
     cells_x, cells_y, cells_z = solid_ref.shape
     b, s = lax.axis_index("brick"), lax.axis_index("sub")
     hi, y = s // ny, lax.rem(s, ny)
-    other = 1 - hi
-    partner = (b, other * ny + y)
+    partner = (b, (1 - hi) * ny + y)
+    lead, late = hi == 0, hi != 0
 
     def at(db, ds):
         return (lax.rem(b + db + nb, nb), lax.rem(s + ds + ns, ns))
 
     def ring(k):
-        return (b, hi * ny + lax.rem(y + k, ny))
+        return (b, lax.rem(y + k, ny))
 
     def copy(src, dst, send, recv, device):
         return pltpu.make_async_remote_copy(
@@ -242,6 +243,14 @@
         pl.semaphore_signal(barrier, inc=1, device_id=at(0, k), device_id_type=MESH)
     for _, cx, cy in CORNERS:
         pl.semaphore_signal(barrier, inc=1, device_id=at(cx, cy), device_id_type=MESH)
+
+    @pl.when(late)
+    def _():
+        def greet_lead(k, carry):
+            pl.semaphore_signal(barrier, inc=1, device_id=(lax.rem(b + k, nb), y), device_id_type=MESH)
+            return carry
+
+        lax.fori_loop(1, nb, greet_lead, 0)
 
     loads = [
         pltpu.make_async_copy(src, dst, load_s.at[n])
@@ -374,7 +383,7 @@
         gbuf[0, 6:8, :] = jnp.zeros((2, junctions), F32)
 
     def prepare_lattice():
-        for n in (0, 1, 2, 3):
+        for n in (1, 2):
             loads[n].wait()
         hits = hit()
         found = jnp.sum(jnp.where(hits, 1.0, 0.0), axis=1, keepdims=True)
@@ -387,7 +396,7 @@
         pack()
 
     def prepare_messages():
-        for n in (4, 5):
+        for n in (3, 4, 5, 0):
             loads[n].wait()
         dest = dest_ref[...]
         eye = iota((blocks, blocks), 0) == iota((blocks, blocks), 1)
@@ -429,75 +438,88 @@
     def prepare_network():
         for n in (6, 7, 8, 10):
             loads[n].wait()
-        ptab[s] = segp_ref[...]
-        rates[s] = stage[...]
-        build(0, mem_ref)
+
+        @pl.when(lead)
+        def _():
+            build(0, mem_ref)
+
         loads[9].wait()
         high, low = split2(w_ref[...])
         w_parts[:, 0:cells_z] = high
         w_parts[:, cells_z : 2 * cells_z] = low
         w_parts[:, 2 * cells_z : 3 * cells_z] = high
 
+    def spread(src, dst, send, recv):
+        near = [copy(src, dst, send.at[k], recv.at[k], ring(k)) for k in range(1, ny)]
+        far = [copy(src, dst, send.at[k], recv.at[ny + k], ring(k)) for k in range(ny)]
+        return near, far
+
     pair = [
         copy(mem_hbm, other_mem, pair_s.at[0], pair_r.at[0], partner),
         copy(gbuf.at[0], gbuf.at[1], pair_s.at[1], pair_r.at[1], partner),
+        copy(labels.at[0], labels.at[1], pair_s.at[2], pair_r.at[2], partner),
+        copy(ptab.at[ny + y], last, pair_s.at[3], pair_r.at[3], partner),
     ]
-    first = [
-        copy(segp_hbm, ptab.at[s], first_s.at[k - 1], first_r.at[k - 1], at(0, k)) for k in range(1, ns)
-    ]
-    second = [
-        copy(stage, rates.at[s], rates_s.at[k - 1], rates_r.at[k - 1], at(0, k)) for k in range(1, ns)
-    ]
+    first = spread(segp_hbm, ptab.at[s], first_s, first_r)
+    second = spread(stage, rates.at[s], rates_s, rates_r)
+    third = spread(flow, inflow_all.at[s], inflow_s, inflow_r)
 
     def message(k):
         target = lax.rem(b + k, nb)
         return copy(msg.at[target], arrived.at[b], msg_s, msg_r, (target, s))
 
-    def answer(k):
+    def answer(k, n):
         target = lax.rem(b + k, nb)
-        return copy(ret_out.at[target], ret_in.at[b], ret_s, ret_r, (target, s))
+        return copy(ret_out.at[n, target], ret_in.at[b], ret_s.at[n], ret_r, (target, n * ny + y))
 
     def start_message(k, carry):
         message(lax.rem(k + nb // 4, nb - 1) + 1).start()
         return carry
 
-    early, late = hi == 0, hi != 0
-
-    @pl.when(early)
-    def _():
+    @pl.when(lead)
+    def _():
+        prepare_messages()
         prepare_junctions()
         prepare_lattice()
-        prepare_messages()
         prepare_network()
-
-    pl.semaphore_wait(barrier, nb - 1 + ns - 1 + len(CORNERS))
-
-    pair[0].start()
-    for c in first:
-        c.start()
+        ptab[s] = segp_ref[...]
+        rates[s] = stage[...]
+
+    pl.semaphore_wait(barrier, nb - 1 + ns - 1 + len(CORNERS) + jnp.where(lead, nb - 1, 0))
 
     @pl.when(late)
     def _():
+        pair[0].start()
+        for c in first[1]:
+            c.start()
         prepare_junctions()
-
-    pair[1].start()
-
-    @pl.when(late)
-    def _():
-        prepare_lattice()
-
-    start_halo(0)
-
-    @pl.when(late)
-    def _():
+        pair[1].start()
         prepare_messages()
 
     lax.fori_loop(1, nb, start_message, 0)
     arrived[b] = msg[b]
 
+    @pl.when(lead)
+    def _():
+        for c in first[0]:
+            c.start()
+
     @pl.when(late)
     def _():
+        prepare_lattice()
+
+    start_halo(0)
+
+    @pl.when(lead)
+    def _():
+        for c in second[0]:
+            c.start()
+
+    @pl.when(late)
+    def _():
         prepare_network()
+        for c in second[1]:
+            c.start()
 
     def flows(n, table):
         members = oh_c[n]
@@ -520,20 +542,18 @@
             preferred_element_type=F32,
         )
 
+    def numbers_of(n):
+        rows_of = jnp.broadcast_to(labels[n], (nb, 4, 128)).reshape(nb * 4, 128)
+        at_row = iota((nb * 4, 128), 0) & 3
+        number = jnp.sum(jnp.where(iota((nb * 4, 128), 1) == at_row, rows_of, 0.0), axis=1, keepdims=True)
+        return jnp.where(at_row < SLOTS, jnp.broadcast_to(number.astype(jnp.int32), (nb * 4, 128)), -1)
+
     def inflows():
         whole = pl.ds(0, nb - 1)
         copy(msg.at[whole], arrived.at[whole], msg_s, msg_r, at(1, 0)).wait()
         got = arrived[...].reshape(nb * 4, cells_z)
-        at_row = iota((nb * 4, cells_z), 0) & 3
-        labels = jnp.where(
-            at_row == 0,
-            pltpu.roll(got, nb * 4 - 3, 0),
-            jnp.where(at_row == 1, pltpu.roll(got, nb * 4 - 2, 0), pltpu.roll(got, nb * 4 - 1, 0)),
-        )
-        labels = jnp.where(iota((nb * 4, cells_z), 1) == at_row, labels, 0.0)
-        numbers = jnp.sum(labels, axis=1, keepdims=True).astype(jnp.int32)
-        numbers = jnp.where(at_row < SLOTS, jnp.broadcast_to(numbers, (nb * 4, 128)), -1)
-        ids_ref[...] = numbers
+        labels[0] = arrived[:, 3:4, :]
+        numbers = numbers_of(0)
         lane = iota((nb * 4, 128), 1)
         high, low = split2(got)
         value = lax.dot_general(
@@ -545,17 +565,18 @@
         for n in range(rows):
             mine = jnp.where(numbers == lane + n * 128, value[:, n * 128 : (n + 1) * 128], 0.0)
             flow[n : n + 1, :] = jnp.sum(mine, axis=0, keepdims=True)
-        third = [
-            copy(flow, inflow_all.at[s], inflow_s.at[k - 1], inflow_r.at[k - 1], at(0, k))
-            for k in range(1, ns)
-        ]
-        for c in third:
-            c.start()
-        inflow_all[s] = flow[...]
-        for c in second:
-            c.wait()
-        for c in third:
-            c.wait()
+
+        @pl.when(lead)
+        def _():
+            for c in third[0]:
+                c.start()
+            inflow_all[s] = flow[...]
+
+        @pl.when(late)
+        def _():
+            for c in third[1]:
+                c.start()
+            pair[2].start()
 
     def table_of():
         return jnp.concatenate(split2(ptab[...].reshape(ns * rows, 128)), axis=1)
@@ -563,17 +584,22 @@
     def joined(both):
         return both[:, :128] + both[:, 128:]
 
-    for c in first:
-        c.wait()
-    table = table_of()
-    both = flows(0, table)
-    pair[0].wait()
-    build(1, other_mem)
-    pair[1].wait()
-    for c in second:
-        c.start()
-    both = both + flows(1, table)
-    part[0, y] = joined(both)
+    def arrive(copies):
+        for c in copies[0]:
+            c.wait()
+        for c in copies[1]:
+            c.wait_recv()
+
+    @pl.when(lead)
+    def _():
+        arrive(first)
+        table = table_of()
+        both = flows(0, table)
+        pair[0].wait_recv()
+        build(1, other_mem)
+        pair[1].wait_recv()
+        both = both + flows(1, table)
+        part[0, y] = joined(both)
 
     def step(t, carry):
         parity = lax.rem(t, 2)
@@ -581,8 +607,15 @@
             copy(part.at[parity, y], part.at[parity, y], part_s.at[k - 1], part_r.at[parity, k - 1], ring(k))
             for k in range(1, ny)
         ]
-        for c in partial:
-            c.start()
+
+        @pl.when(lead)
+        def _():
+            for c in partial:
+                c.start()
+
+        @pl.when(t == 0)
+        def _():
+            inflows()
 
         now = halo(parity)
         for c in now:
@@ -597,48 +630,73 @@
             pack()
             start_halo(1 - parity)
 
-        @pl.when(t == 0)
+        @pl.when(lead)
         def _():
-            inflows()
-
-        for c in partial:
-            c.wait()
-        balance = part[parity, 0]
-        for k in range(1, ny):
-            balance = balance + part[parity, k]
-        p = ptab[...].reshape(ns * rows, 128)
-        rate = rates[:, 0].reshape(ns * rows, 128)
-        leak = rates[:, 1].reshape(ns * rows, 128)
-        source = inflow_all[...].reshape(ns * rows, 128)
-        ptab[...] = (p + rate * (source - balance - leak * p)).reshape(ns, rows, 128)
-
-        @pl.when(t < STEPS - 1)
-        def _():
-            table = table_of()
-            part[1 - parity, y] = joined(flows(0, table) + flows(1, table))
+            for c in partial:
+                c.wait()
+
+            @pl.when(t == 0)
+            def _():
+                arrive(second)
+                arrive(third)
+
+            balance = part[parity, 0]
+            for k in range(1, ny):
+                balance = balance + part[parity, k]
+            p = ptab[...].reshape(ns * rows, 128)
+            rate = rates[:, 0].reshape(ns * rows, 128)
+            leak = rates[:, 1].reshape(ns * rows, 128)
+            source = inflow_all[...].reshape(ns * rows, 128)
+            ptab[...] = (p + rate * (source - balance - leak * p)).reshape(ns, rows, 128)
+
+            @pl.when(t < STEPS - 1)
+            def _():
+                table = table_of()
+                part[1 - parity, y] = joined(flows(0, table) + flows(1, table))
 
         return carry
 
     lax.fori_loop(0, STEPS, step, 0)
-    final = ptab[s]
-    seg_out[...] = final
-
-    numbers = ids_ref[...]
-    lane = iota((nb * 4, 128), 1)
-    value = jnp.zeros((nb * 4, 128), F32)
-    for n in range(rows):
-        value = value + jnp.where(numbers == lane + n * 128, final[n : n + 1, :], 0.0)
-    value = jnp.sum(value, axis=1, keepdims=True)
-    ret_out[...] = jnp.broadcast_to(value, (nb * 4, 128)).reshape(nb, 4, 128)
-
-    def start_answer(k, carry):
-        answer(lax.rem(k + nb // 4, nb - 1) + 1).start()
-        return carry
-
-    lax.fori_loop(1, nb, start_answer, 0)
-    ret_in[b] = ret_out[b]
+
     whole = pl.ds(0, nb - 1)
-    copy(ret_out.at[whole], ret_in.at[whole], ret_s, ret_r, at(1, 0)).wait()
+
+    @pl.when(lead)
+    def _():
+        pair[3].start()
+        pair[2].wait_recv()
+        lane = iota((nb * 4, 128), 1)
+        for n in (1, 0):
+            final = ptab[n * ny + y]
+            numbers = numbers_of(n)
+            value = jnp.zeros((nb * 4, 128), F32)
+            for line in range(rows):
+                value = value + jnp.where(numbers == lane + line * 128, final[line : line + 1, :], 0.0)
+            value = jnp.sum(value, axis=1, keepdims=True)
+            ret_out[n] = jnp.broadcast_to(value, (nb * 4, 128)).reshape(nb, 4, 128)
+
+            def start_answer(k, carry):
+                answer(lax.rem(k + nb // 4, nb - 1) + 1, n).start()
+                return carry
+
+            lax.fori_loop(1, nb, start_answer, 0)
+        answer(0, 1).start()
+        ret_in[b] = ret_out[0, b]
+        seg_out[...] = ptab[y]
+        copy(ret_out.at[0, whole], ret_in.at[whole], ret_s.at[0], ret_r, at(1, 0)).wait()
+        copy(ret_out.at[1], ret_in, ret_s.at[1], ret_r, at(1, 0)).wait_send()
+        pair[3].wait_send()
+
+    @pl.when(late)
+    def _():
+        for copies in (first, second, third):
+            for c in copies[1]:
+                c.wait_send()
+        for c in pair[:3]:
+            c.wait_send()
+        pair[3].wait_recv()
+        seg_out[...] = last[...]
+        copy(ret_out.at[1], ret_in, ret_s.at[1], ret_r, at(1, 0)).wait_recv()
+
     back = ret_in[...].reshape(nb * 4, 128)[:, :blocks]
     bp_out[...] = jnp.sum(jnp.where(pick[...] > 0.5, back, 0.0), axis=0, keepdims=True)
 
@@ -716,25 +774,26 @@
         vmem((nb, 4, cz), F32),
         vmem((nb, 4, cz), F32),
         vmem((nb * 4, blocks), F32),
-        vmem((nb * 4, cz), jnp.int32),
+        vmem((2, nb, 1, 128), F32),
+        vmem((rows, 128), F32),
         vmem((segs, 3 * cz), BF16),
-        vmem((nb, 4, 128), F32),
+        vmem((2, nb, 4, 128), F32),
         vmem((nb, 4, 128), F32),
         dma((8,)),
         dma((2, 8)),
-        dma((ns - 1,)),
-        dma((ns - 1,)),
-        dma((ns - 1,)),
-        dma((ns - 1,)),
-        dma((ns - 1,)),
-        dma((ns - 1,)),
-        dma((2,)),
-        dma((2,)),
+        dma((ny,)),
+        dma((ns,)),
+        dma((ny,)),
+        dma((ns,)),
+        dma((ny,)),
+        dma((ns,)),
+        dma((4,)),
+        dma((4,)),
         dma((ny - 1,)),
         dma((2, ny - 1)),
         dma,
         dma,
-        dma,
+        dma((2,)),
         dma,
     ]
     spec = pl.BlockSpec(memory_space=vmem)

time: 76.2 us -> 73.8 us (0.969)
  Pallas kernels: 75.4 us -> 73 us
    pallas_call x1, Pallas kernels: 74.4 us -> 72 us  [local(): pl.pallas_call(functools.partial(kernel, nb, ns), out_shape=(pltpu.VMEM(p...]
where the time goes in v4:
time: 73.8 us; the launch traced here: 73.7 us
  Pallas kernels  73 us (99%)
    pallas_call x1, Pallas kernels, local(): pl.pallas_call(functools.partial(kernel, nb, ns), out_shape=(pltpu.VMEM(p...  72 us

profile of v4, /device:TPU:1, one launch (start us, length us, event | category | flops | bytes accessed | tf_op | source)
XLA Modules:
  0.0 73.7 jit_solution(2090119076004760202)
XLA Ops:
  0.6 72.0 %coupled.1 = (f32[19,4,16,128]{3,2,1,0:T(8,128)S(1)}, f32[16,128]{1,0:T(8,128)S(1)}, f32[1,32]{1,0:T(1,128)S(1)}) custom-call(f32[19,4,16,128]{3,2,1,0:T(8,128)} %pop_hbm.1, s32[4,16,128]{2,1,0:T(8,128)} %solid_hbm.1, f32[1,32]{1,0:T(1,128)} %bitcast.14, s32[1,32]{1,0:T(1,128)} %bitcast.15, s32[1,32]{1,0:T(1,128)} %bitcast.16, s32[1,32]{1,0:T(1,128)} %bitcast.17, ...), custom_call_target="tpu_custom_call" | custom-call | tf_op jit(solution)/shard_map/coupled/pallas_call | solution.py:800
  72.7 1.0 %finish.1 = (f32[19,4,16,128]{3,2,1,0:T(8,128)}, f32[16,128]{1,0:T(8,128)}, f32[1,32]{1,0:T(1,128)}) custom-call(f32[19,4,16,128]{3,2,1,0:T(8,128)S(1)} %get-tuple-element.9.pop_in, f32[16,128]{1,0:T(8,128)S(1)} %get-tuple-element.10.seg_in, f32[1,32]{1,0:T(1,128)S(1)} %get-tuple-element.11.bp_in), custom_call_target="tpu_custom_call" | custom-call | tf_op jit(solution)/shard_map/finish/pallas_call | solution.py:831

commit v5 on v4

--- a/solution.py
+++ b/solution.py
@@ -189,6 +189,7 @@
     arrived,
     pick,
     labels,
+    numbers_ref,
     last,
     w_parts,
     ret_out,
@@ -217,40 +218,20 @@
     blocks = col_ref.shape[1]
     cells_x, cells_y, cells_z = solid_ref.shape
     b, s = lax.axis_index("brick"), lax.axis_index("sub")
-    hi, y = s // ny, lax.rem(s, ny)
+    hi, y = s // ny, s & (ny - 1)
     partner = (b, (1 - hi) * ny + y)
     lead, late = hi == 0, hi != 0
 
     def at(db, ds):
-        return (lax.rem(b + db + nb, nb), lax.rem(s + ds + ns, ns))
+        return ((b + db) & (nb - 1), (s + ds) & (ns - 1))
 
     def ring(k):
-        return (b, lax.rem(y + k, ny))
+        return (b, (y + k) & (ny - 1))
 
     def copy(src, dst, send, recv, device):
         return pltpu.make_async_remote_copy(
             src_ref=src, dst_ref=dst, send_sem=send, recv_sem=recv, device_id=device, device_id_type=MESH
         )
-
-    barrier = pltpu.get_barrier_semaphore()
-
-    def greet(k, carry):
-        pl.semaphore_signal(barrier, inc=1, device_id=at(k, 0), device_id_type=MESH)
-        return carry
-
-    lax.fori_loop(1, nb, greet, 0)
-    for k in range(1, ns):
-        pl.semaphore_signal(barrier, inc=1, device_id=at(0, k), device_id_type=MESH)
-    for _, cx, cy in CORNERS:
-        pl.semaphore_signal(barrier, inc=1, device_id=at(cx, cy), device_id_type=MESH)
-
-    @pl.when(late)
-    def _():
-        def greet_lead(k, carry):
-            pl.semaphore_signal(barrier, inc=1, device_id=(lax.rem(b + k, nb), y), device_id_type=MESH)
-            return carry
-
-        lax.fori_loop(1, nb, greet_lead, 0)
 
     loads = [
         pltpu.make_async_copy(src, dst, load_s.at[n])
@@ -275,6 +256,21 @@
     ]
     for n in (11, 12, 13, 4, 5, 3, 2, 0, 10, 6, 7, 8, 1, 9):
         loads[n].start()
+
+    barrier = pltpu.get_barrier_semaphore()
+
+    for k in range(1, nb):
+        pl.semaphore_signal(barrier, inc=1, device_id=at(k, 0), device_id_type=MESH)
+    for k in range(1, ns):
+        pl.semaphore_signal(barrier, inc=1, device_id=at(0, k), device_id_type=MESH)
+    for _, cx, cy in CORNERS:
+        pl.semaphore_signal(barrier, inc=1, device_id=at(cx, cy), device_id_type=MESH)
+
+    @pl.when(late)
+    def _():
+        for k in range(1, nb):
+            pl.semaphore_signal(barrier, inc=1, device_id=(at(k, 0)[0], y), device_id_type=MESH)
+
 
     def halo(parity):
         copies = [
@@ -465,16 +461,14 @@
     third = spread(flow, inflow_all.at[s], inflow_s, inflow_r)
 
     def message(k):
-        target = lax.rem(b + k, nb)
+        target = (b + k) & (nb - 1)
         return copy(msg.at[target], arrived.at[b], msg_s, msg_r, (target, s))
 
     def answer(k, n):
-        target = lax.rem(b + k, nb)
+        target = (b + k) & (nb - 1)
         return copy(ret_out.at[n, target], ret_in.at[b], ret_s.at[n], ret_r, (target, n * ny + y))
 
-    def start_message(k, carry):
-        message(lax.rem(k + nb // 4, nb - 1) + 1).start()
-        return carry
+    order = [(k + nb // 4) % (nb - 1) + 1 for k in range(1, nb)]
 
     @pl.when(lead)
     def _():
@@ -496,7 +490,8 @@
         pair[1].start()
         prepare_messages()
 
-    lax.fori_loop(1, nb, start_message, 0)
+    for k in order:
+        message(k).start()
     arrived[b] = msg[b]
 
     @pl.when(lead)
@@ -554,6 +549,7 @@
         got = arrived[...].reshape(nb * 4, cells_z)
         labels[0] = arrived[:, 3:4, :]
         numbers = numbers_of(0)
+        numbers_ref[0] = numbers
         lane = iota((nb * 4, 128), 1)
         high, low = split2(got)
         value = lax.dot_general(
@@ -630,6 +626,11 @@
             pack()
             start_halo(1 - parity)
 
+        @pl.when(jnp.logical_and(lead, t == 1))
+        def _():
+            pair[2].wait_recv()
+            numbers_ref[1] = numbers_of(1)
+
         @pl.when(lead)
         def _():
             for c in partial:
@@ -663,22 +664,18 @@
     @pl.when(lead)
     def _():
         pair[3].start()
-        pair[2].wait_recv()
         lane = iota((nb * 4, 128), 1)
         for n in (1, 0):
             final = ptab[n * ny + y]
-            numbers = numbers_of(n)
+            numbers = numbers_ref[n]
             value = jnp.zeros((nb * 4, 128), F32)
             for line in range(rows):
                 value = value + jnp.where(numbers == lane + line * 128, final[line : line + 1, :], 0.0)
             value = jnp.sum(value, axis=1, keepdims=True)
             ret_out[n] = jnp.broadcast_to(value, (nb * 4, 128)).reshape(nb, 4, 128)
 
-            def start_answer(k, carry):
-                answer(lax.rem(k + nb // 4, nb - 1) + 1, n).start()
-                return carry
-
-            lax.fori_loop(1, nb, start_answer, 0)
+            for k in order:
+                answer(k, n).start()
         answer(0, 1).start()
         ret_in[b] = ret_out[0, b]
         seg_out[...] = ptab[y]
@@ -775,6 +772,7 @@
         vmem((nb, 4, cz), F32),
         vmem((nb * 4, blocks), F32),
         vmem((2, nb, 1, 128), F32),
+        vmem((2, nb * 4, 128), jnp.int32),
         vmem((rows, 128), F32),
         vmem((segs, 3 * cz), BF16),
         vmem((2, nb, 4, 128), F32),

time: 73.8 us -> 72.5 us (0.982)
  Pallas kernels: 73 us -> 71.8 us
    pallas_call x1, Pallas kernels: 72 us -> 70.8 us  [local(): pl.pallas_call(functools.partial(kernel, nb, ns), out_shape=(pltpu.VMEM(p...]
where the time goes in v5:
time: 72.5 us; the launch traced here: 72.4 us
  Pallas kernels  71.8 us (99%)
    pallas_call x1, Pallas kernels, local(): pl.pallas_call(functools.partial(kernel, nb, ns), out_shape=(pltpu.VMEM(p...  70.8 us

profile of v5, /device:TPU:1, one launch (start us, length us, event | category | flops | bytes accessed | tf_op | source)
XLA Modules:
  0.0 72.4 jit_solution(16633892986677473549)
XLA Ops:
  0.6 70.8 %coupled.1 = (f32[19,4,16,128]{3,2,1,0:T(8,128)S(1)}, f32[16,128]{1,0:T(8,128)S(1)}, f32[1,32]{1,0:T(1,128)S(1)}) custom-call(f32[19,4,16,128]{3,2,1,0:T(8,128)} %pop_hbm.1, s32[4,16,128]{2,1,0:T(8,128)} %solid_hbm.1, f32[1,32]{1,0:T(1,128)} %bitcast.14, s32[1,32]{1,0:T(1,128)} %bitcast.15, s32[1,32]{1,0:T(1,128)} %bitcast.16, s32[1,32]{1,0:T(1,128)} %bitcast.17, ...), custom_call_target="tpu_custom_call" | custom-call | tf_op jit(solution)/shard_map/coupled/pallas_call | solution.py:798
  71.4 1.0 %finish.1 = (f32[19,4,16,128]{3,2,1,0:T(8,128)}, f32[16,128]{1,0:T(8,128)}, f32[1,32]{1,0:T(1,128)}) custom-call(f32[19,4,16,128]{3,2,1,0:T(8,128)S(1)} %get-tuple-element.9.pop_in, f32[16,128]{1,0:T(8,128)S(1)} %get-tuple-element.10.seg_in, f32[1,32]{1,0:T(1,128)S(1)} %get-tuple-element.11.bp_in), custom_call_target="tpu_custom_call" | custom-call | tf_op jit(solution)/shard_map/finish/pallas_call | solution.py:829

commit v6 on v5

--- a/solution.py
+++ b/solution.py
@@ -206,6 +206,8 @@
     pair_r,
     part_s,
     part_r,
+    tail_s,
+    tail_r,
     msg_s,
     msg_r,
     ret_s,
@@ -604,9 +606,22 @@
             for k in range(1, ny)
         ]
 
-        @pl.when(lead)
+        tail = []
+        for k in range(1, ny):
+            target = (y + k) & (ny - 1)
+            for n in range(2):
+                lines = pl.ds(pl.multiple_of((n * ny + target) * rows, rows), rows)
+                piece = part.at[parity, y, lines]
+                tail.append(copy(piece, piece, tail_s.at[k - 1, n], tail_r.at[k - 1, n], ring(k)))
+
+        @pl.when(jnp.logical_and(lead, t < STEPS - 1))
         def _():
             for c in partial:
+                c.start()
+
+        @pl.when(jnp.logical_and(lead, t == STEPS - 1))
+        def _():
+            for c in tail:
                 c.start()
 
         @pl.when(t == 0)
@@ -631,11 +646,18 @@
             pair[2].wait_recv()
             numbers_ref[1] = numbers_of(1)
 
-        @pl.when(lead)
+        @pl.when(jnp.logical_and(lead, t < STEPS - 1))
         def _():
             for c in partial:
                 c.wait()
 
+        @pl.when(jnp.logical_and(lead, t == STEPS - 1))
+        def _():
+            for c in tail:
+                c.wait()
+
+        @pl.when(lead)
+        def _():
             @pl.when(t == 0)
             def _():
                 arrive(second)
@@ -789,6 +811,8 @@
         dma((4,)),
         dma((ny - 1,)),
         dma((2, ny - 1)),
+        dma((ny - 1, 2)),
+        dma((ny - 1, 2)),
         dma,
         dma,
         dma((2,)),

time: 72.5 us -> 71.6 us (0.988)
  Pallas kernels: 71.8 us -> 70.8 us
    pallas_call x1, Pallas kernels: 70.8 us -> 69.8 us  [local(): pl.pallas_call(functools.partial(kernel, nb, ns), out_shape=(pltpu.VMEM(p...]
where the time goes in v6:
time: 71.6 us; the launch traced here: 71.5 us
  Pallas kernels  70.8 us (99%)
    pallas_call x1, Pallas kernels, local(): pl.pallas_call(functools.partial(kernel, nb, ns), out_shape=(pltpu.VMEM(p...  69.8 us

profile of v6, /device:TPU:1, one launch (start us, length us, event | category | flops | bytes accessed | tf_op | source)
XLA Modules:
  0.0 71.5 jit_solution(15617803772713090012)
XLA Ops:
  0.6 69.8 %coupled.1 = (f32[19,4,16,128]{3,2,1,0:T(8,128)S(1)}, f32[16,128]{1,0:T(8,128)S(1)}, f32[1,32]{1,0:T(1,128)S(1)}) custom-call(f32[19,4,16,128]{3,2,1,0:T(8,128)} %pop_hbm.1, s32[4,16,128]{2,1,0:T(8,128)} %solid_hbm.1, f32[1,32]{1,0:T(1,128)} %bitcast.14, s32[1,32]{1,0:T(1,128)} %bitcast.15, s32[1,32]{1,0:T(1,128)} %bitcast.16, s32[1,32]{1,0:T(1,128)} %bitcast.17, ...), custom_call_target="tpu_custom_call" | custom-call | tf_op jit(solution)/shard_map/coupled/pallas_call | solution.py:822
  70.5 1.0 %finish.1 = (f32[19,4,16,128]{3,2,1,0:T(8,128)}, f32[16,128]{1,0:T(8,128)}, f32[1,32]{1,0:T(1,128)}) custom-call(f32[19,4,16,128]{3,2,1,0:T(8,128)S(1)} %get-tuple-element.9.pop_in, f32[16,128]{1,0:T(8,128)S(1)} %get-tuple-element.10.seg_in, f32[1,32]{1,0:T(1,128)S(1)} %get-tuple-element.11.bp_in), custom_call_target="tpu_custom_call" | custom-call | tf_op jit(solution)/shard_map/finish/pallas_call | solution.py:853

commit v7 on v6

--- a/solution.py
+++ b/solution.py
@@ -616,8 +616,8 @@
 
         @pl.when(jnp.logical_and(lead, t < STEPS - 1))
         def _():
-            for c in partial:
-                c.start()
+            for k in (1, 0, 2):
+                partial[k].start()
 
         @pl.when(jnp.logical_and(lead, t == STEPS - 1))
         def _():

time: 71.6 us -> 69.9 us (0.976)
  Pallas kernels: 70.8 us -> 69.2 us
    pallas_call x1, Pallas kernels: 69.8 us -> 68.2 us  [local(): pl.pallas_call(functools.partial(kernel, nb, ns), out_shape=(pltpu.VMEM(p...]
where the time goes in v7:
time: 69.9 us; the launch traced here: 69.8 us
  Pallas kernels  69.2 us (99%)
    pallas_call x1, Pallas kernels, local(): pl.pallas_call(functools.partial(kernel, nb, ns), out_shape=(pltpu.VMEM(p...  68.2 us

profile of v7, /device:TPU:1, one launch (start us, length us, event | category | flops | bytes accessed | tf_op | source)
XLA Modules:
  0.0 69.8 jit_solution(12097180424700437234)
XLA Ops:
  0.6 68.2 %coupled.1 = (f32[19,4,16,128]{3,2,1,0:T(8,128)S(1)}, f32[16,128]{1,0:T(8,128)S(1)}, f32[1,32]{1,0:T(1,128)S(1)}) custom-call(f32[19,4,16,128]{3,2,1,0:T(8,128)} %pop_hbm.1, s32[4,16,128]{2,1,0:T(8,128)} %solid_hbm.1, f32[1,32]{1,0:T(1,128)} %bitcast.14, s32[1,32]{1,0:T(1,128)} %bitcast.15, s32[1,32]{1,0:T(1,128)} %bitcast.16, s32[1,32]{1,0:T(1,128)} %bitcast.17, ...), custom_call_target="tpu_custom_call" | custom-call | tf_op jit(solution)/shard_map/coupled/pallas_call | solution.py:822
  68.8 1.0 %finish.1 = (f32[19,4,16,128]{3,2,1,0:T(8,128)}, f32[16,128]{1,0:T(8,128)}, f32[1,32]{1,0:T(1,128)}) custom-call(f32[19,4,16,128]{3,2,1,0:T(8,128)S(1)} %get-tuple-element.9.pop_in, f32[16,128]{1,0:T(8,128)S(1)} %get-tuple-element.10.seg_in, f32[1,32]{1,0:T(1,128)S(1)} %get-tuple-element.11.bp_in), custom_call_target="tpu_custom_call" | custom-call | tf_op jit(solution)/shard_map/finish/pallas_call | solution.py:853

commit v8 on v7

--- a/solution.py
+++ b/solution.py
@@ -649,7 +649,7 @@
         @pl.when(jnp.logical_and(lead, t < STEPS - 1))
         def _():
             for c in partial:
-                c.wait()
+                c.wait_recv()
 
         @pl.when(jnp.logical_and(lead, t == STEPS - 1))
         def _():
@@ -676,6 +676,8 @@
             def _():
                 table = table_of()
                 part[1 - parity, y] = joined(flows(0, table) + flows(1, table))
+                for c in partial:
+                    c.wait_send()
 
         return carry
 

time: 69.9 us -> 70 us (level)
  no operation moved by 1% of the time
where the time goes in v8:
time: 70 us; the launch traced here: 69.9 us
  Pallas kernels  69.2 us (99%)
    pallas_call x1, Pallas kernels, local(): pl.pallas_call(functools.partial(kernel, nb, ns), out_shape=(pltpu.VMEM(p...  68.2 us

profile of v8, /device:TPU:1, one launch (start us, length us, event | category | flops | bytes accessed | tf_op | source)
XLA Modules:
  0.0 69.9 jit_solution(1472563509715811718)
XLA Ops:
  0.6 68.2 %coupled.1 = (f32[19,4,16,128]{3,2,1,0:T(8,128)S(1)}, f32[16,128]{1,0:T(8,128)S(1)}, f32[1,32]{1,0:T(1,128)S(1)}) custom-call(f32[19,4,16,128]{3,2,1,0:T(8,128)} %pop_hbm.1, s32[4,16,128]{2,1,0:T(8,128)} %solid_hbm.1, f32[1,32]{1,0:T(1,128)} %bitcast.14, s32[1,32]{1,0:T(1,128)} %bitcast.15, s32[1,32]{1,0:T(1,128)} %bitcast.16, s32[1,32]{1,0:T(1,128)} %bitcast.17, ...), custom_call_target="tpu_custom_call" | custom-call | tf_op jit(solution)/shard_map/coupled/pallas_call | solution.py:824
  68.9 1.0 %finish.1 = (f32[19,4,16,128]{3,2,1,0:T(8,128)}, f32[16,128]{1,0:T(8,128)}, f32[1,32]{1,0:T(1,128)}) custom-call(f32[19,4,16,128]{3,2,1,0:T(8,128)S(1)} %get-tuple-element.9.pop_in, f32[16,128]{1,0:T(8,128)S(1)} %get-tuple-element.10.seg_in, f32[1,32]{1,0:T(1,128)S(1)} %get-tuple-element.11.bp_in), custom_call_target="tpu_custom_call" | custom-call | tf_op jit(solution)/shard_map/finish/pallas_call | solution.py:855
